TPU v7x, 128 devices: a whole 4x4x4 slice. The times are simulated.
128 devices in a mesh: ctx: 32 (over y_hi, z, x), cand: 4 (over y_lo, core).
Axes of the slice: x: 4, y: 4 (y_hi: 2, y_lo: 2; y = y_hi * 2 + y_lo), z: 4, core: 2. Of those that a mesh axis runs over, the one named last changes fastest.
Arguments:
- history: bfloat16 [32768, 1024], P('ctx'), may hold values from -6 to 6
- candidates: bfloat16 [4096, 1024], P('ctx'), may hold values from -6 to 6
- history_valid: int32 [32768], P('ctx'), may hold values 0 or 1
- history_surface: int32 [32768], P('ctx'), may hold values from 0 to 7
- candidate_surface: int32 [4096], P('ctx'), may hold values from 0 to 7
- candidate_cutoff: int32 [4096], P('ctx'), may hold values from 1 to 32768
- gain_in: float32 [1024], replicated, may hold values from 0.1 to 1.9
- w_uvqk: bfloat16 [1024, 4, 1024], P(None, None, 'cand'), may hold values from -0.1875 to 0.1875
- gain_out: float32 [1024], P('cand'), may hold values from 0.1 to 1.9
- w_out: bfloat16 [1024, 1024], P('cand'), may hold values from -0.25 to 0.25
Outputs:
- history_out: bfloat16 [32768, 1024], P('ctx', 'cand')
- candidate_out: bfloat16 [4096, 1024], P('ctx', 'cand')
All inputs are finite; a program needn't handle non-finite values. No bound on the sum of `history_valid` on one device may be relied on, other than what follows from the above.
Results may differ from a plain program's by a relative error of at most 0.0062.
Values may be sent and summed in bfloat16 or wider, within the bound.
A program may use at most 128 MiB of HBM per device.

v0:
```python
import math

import jax
import jax.numpy as jnp
from jax import lax
from jax.sharding import PartitionSpec as P

HEAD = 128


EPS = 1e-05


def from_behind(block, axis, distance):
    devices = range(lax.axis_size(axis))
    route = [(i - distance, i) for i in devices if i - distance in devices]
    return lax.ppermute(block, axis, route)


def layer_in(inputs, gain):
    values_f = inputs.astype(jnp.float32)
    center = values_f - jnp.mean(values_f, axis=-1, keepdims=True)
    spread = jnp.mean(center * center, axis=-1, keepdims=True)
    return (center * lax.rsqrt(spread + EPS) * gain).astype(jnp.bfloat16)


def split_heads(matrix):
    return matrix.reshape(matrix.shape[0], matrix.shape[1] // HEAD, HEAD)


def cand_block(queries, cutoff, surface, key_rows, val_rows, okay, key_surface, position):
    scale = 1.0 / math.sqrt(HEAD)
    mask = (
        (okay[None, :] == 1)
        & (position[None, :] < cutoff[:, None])
        & (key_surface[None, :] == surface[:, None])
    )
    scores = (
        jnp.einsum(
            "qhd,khd->hqk",
            split_heads(queries),
            split_heads(key_rows),
            preferred_element_type=jnp.float32,
        )
        * scale
    )
    weights = jnp.where(mask[None], jax.nn.silu(scores), 0.0).astype(jnp.bfloat16)
    summed = jnp.einsum(
        "hqk,khd->qhd", weights, split_heads(val_rows), preferred_element_type=jnp.float32
    )
    return summed.reshape(queries.shape[0], queries.shape[1])


def shards(
    history,
    candidates,
    history_valid,
    history_surface,
    candidate_surface,
    candidate_cutoff,
    gain_in,
    w_uvqk,
    gain_out,
    w_out,
):
    hist_rows = history.shape[0]
    cand_rows = candidates.shape[0]
    local_width = w_uvqk.shape[2]
    scale = 1.0 / math.sqrt(HEAD)
    inputs = jnp.concatenate([history, candidates], 0)
    normed = layer_in(inputs, gain_in)
    flat = w_uvqk.reshape(w_uvqk.shape[0], 4 * local_width)
    proj = jax.nn.silu(jnp.dot(normed, flat, preferred_element_type=jnp.float32)).astype(
        jnp.bfloat16
    )
    proj = proj.reshape(inputs.shape[0], 4, local_width)
    update = proj[:, 0]
    hist_vals = proj[:hist_rows, 1]
    hist_query = proj[:hist_rows, 2]
    hist_keys = proj[:hist_rows, 3]
    cand_vals = proj[hist_rows:, 1]
    cand_query = proj[hist_rows:, 2]
    cand_keys = proj[hist_rows:, 3]
    moving = (hist_keys, hist_vals, history_valid)
    passed = []
    for repeat in range(2):
        moving = from_behind((moving[0], moving[1], moving[2]), "ctx", 1)
        passed.append(moving)
    second_back = passed[1]
    first_back = passed[0]
    window_keys = jnp.concatenate([second_back[0], first_back[0], hist_keys], 0)
    window_vals = jnp.concatenate([second_back[1], first_back[1], hist_vals], 0)
    window_okay = jnp.concatenate([second_back[2], first_back[2], history_valid], 0)
    row_idx = jnp.arange(hist_rows, dtype=jnp.int32)
    col_idx = jnp.arange(3 * hist_rows, dtype=jnp.int32)
    window_mask = (
        (col_idx[None, :] > row_idx[:, None])
        & (col_idx[None, :] <= row_idx[:, None] + 2 * hist_rows)
        & (window_okay[None, :] == 1)
    )
    scores = (
        jnp.einsum(
            "qhd,khd->hqk",
            split_heads(hist_query),
            split_heads(window_keys),
            preferred_element_type=jnp.float32,
        )
        * scale
    )
    weights = jnp.where(window_mask[None], jax.nn.silu(scores), 0.0).astype(jnp.bfloat16)
    hist_attn = jnp.einsum(
        "hqk,khd->qhd", weights, split_heads(window_vals), preferred_element_type=jnp.float32
    )
    hist_attn = hist_attn.reshape(hist_rows, local_width)
    piece = (
        lax.all_gather(hist_keys, "ctx", axis=0, tiled=True),
        lax.all_gather(hist_vals, "ctx", axis=0, tiled=True),
        lax.all_gather(history_valid, "ctx", axis=0, tiled=True),
        lax.all_gather(history_surface, "ctx", axis=0, tiled=True),
    )
    position = jnp.arange(piece[0].shape[0], dtype=jnp.int32)
    cand_attn = cand_block(
        cand_query,
        candidate_cutoff,
        candidate_surface,
        piece[0],
        piece[1],
        piece[2],
        piece[3],
        position,
    )
    self_score = (
        jnp.sum(
            split_heads(cand_query).astype(jnp.float32)
            * split_heads(cand_keys).astype(jnp.float32),
            axis=-1,
        )
        * scale
    )
    self_weight = jax.nn.silu(self_score).astype(jnp.bfloat16).astype(jnp.float32)
    self_term = self_weight[..., None] * split_heads(cand_vals).astype(jnp.float32)
    cand_attn = cand_attn + self_term.reshape(cand_rows, local_width)
    attn = jnp.concatenate([hist_attn, cand_attn], 0)
    row_sums, row_squares = lax.psum(
        (jnp.sum(attn, axis=-1), jnp.sum(attn * attn, axis=-1)), "cand"
    )
    full_width = local_width * lax.axis_size("cand")
    mean_row = (row_sums / full_width)[:, None]
    square_row = (row_squares / full_width)[:, None]
    gated = (
        (attn - mean_row)
        * lax.rsqrt(square_row - mean_row * mean_row + EPS)
        * gain_out
        * update.astype(jnp.float32)
    ).astype(jnp.bfloat16)
    mixed = jnp.dot(gated, w_out, preferred_element_type=jnp.float32)
    shares = lax.psum_scatter(mixed, "cand", scatter_dimension=1, tiled=True)
    out_cols = shares.shape[1]
    residual = lax.dynamic_slice_in_dim(inputs, lax.axis_index("cand") * out_cols, out_cols, 1)
    result = (residual.astype(jnp.float32) + shares).astype(jnp.bfloat16)
    return (result[:hist_rows], result[hist_rows:])


def solution(mesh):
    placed = (
        P("ctx", None),
        P("ctx", None),
        P("ctx"),
        P("ctx"),
        P("ctx"),
        P("ctx"),
        P(),
        P(None, None, "cand"),
        P("cand"),
        P("cand", None),
    )
    return jax.shard_map(
        shards,
        mesh=mesh,
        in_specs=placed,
        out_specs=(P("ctx", "cand"), P("ctx", "cand")),
        check_vma=False,
    )
```

profile of v0, /device:TPU:1, one launch (start us, length us, event | category | flops | bytes accessed | tf_op | source)
XLA Modules:
  0.0 445.5 jit_solution(2883171253697909766)
XLA Ops:
  7.2 1.9 constant_dynamic-update-slice_fusion.1
  9.6 0.8 fusion.9
  10.9 3.6 multiply_convert_fusion
  14.6 1.4 copy-done.2
  16.0 1.6 slice_bitcast_fusion.3
  17.6 0.7 all-gather.7.cloned.1.call-update
  18.4 4.8 %collective-permute-start.4 = (bf16[1024,256]{0,1:T(8,128)(2,1)}, bf16[1024,256]{0,1:T(8,128)(2,1)}, u32[]{:S(2)}, u32[]{:S(2)}) collective-permute-start(bf16[1024,256]{0,1:T(8,128)(2,1)} %get-tuple-element.6), channel_id=1, source_target_pairs={{0,4},{4,8},{8,12},{12,16},{16,20},{20,24},{24,28},{28,32},{32,36}... | collective-permute-start | bytes 1572872 | tf_op jit(solution)/shard_map/ppermute | solution.py:17
  23.2 3.1 collective-permute-start
  26.3 2.0 collective-permute-start.2
  28.3 99.0 %all_gather.13 = s32[32768]{0:T(1024)S(1)} all-gather(s32[1024]{0:T(1024)S(1)} %copy-done.6), channel_id=1, replica_groups=mesh['ctx'=32,'cand'=4] {'ctx'}, dimensions={0}, use_global_device_ids=true | all-gather | bytes 135168 | tf_op jit(solution)/shard_map/all_gather | solution.py:118
  127.3 75.5 %all_gather.14 = s32[32768]{0:T(1024)S(1)} all-gather(s32[1024]{0:T(1024)S(1)} %copy-done.7), channel_id=1, replica_groups=mesh['ctx'=32,'cand'=4] {'ctx'}, dimensions={0}, use_global_device_ids=true | all-gather | bytes 135168 | tf_op jit(solution)/shard_map/all_gather | solution.py:119
  202.8 0.9 fusion.55
  203.8 6.5 %fusion.1 = pred[128,32768]{1,0:T(8,128)(4,1)} fusion(s32[32768]{0:T(1024)S(1)} %all_gather.14, s32[128]{0:T(128)S(1)} %copy-done.9, s32[128]{0:T(128)S(1)} %copy-done.10, pred[32768]{0:T(1024)(128)(4,1)S(1)} %broadcast_compare_fusion), kind=kLoop, calls=%fused_computation.5 | loop fusion | flops 16777216 | bytes 4359168 | tf_op jit(solution)/shard_map/and | solution.py:34
  210.4 3.5 collective-permute-start.3
  213.9 1.0 copy.20
  214.9 4.2 collective-permute-start.5
  219.1 2.1 collective-permute-start.1
  221.2 4.6 %fusion.3 = pred[1024,3072]{1,0:T(8,128)(4,1)} fusion(s32[1024]{0:T(1024)S(1)} %iota_add_fusion, pred[3072]{0:T(1024)(128)(4,1)S(1)} %add_compare_fusion), kind=kLoop, calls=%fused_computation.9 | loop fusion | flops 12582912 | bytes 3152896 | tf_op jit(solution)/shard_map/and | solution.py:97
  225.9 2.0 copy.19
  227.9 6.4 %collective-permute-done.5 = bf16[1024,256]{0,1:T(8,128)(2,1)} collective-permute-done((bf16[1024,256]{0,1:T(8,128)(2,1)}, bf16[1024,256]{0,1:T(8,128)(2,1)}, u32[]{:S(2)}, u32[]{:S(2)}) %collective-permute-start.5) | collective-permute-done | bytes 524320 | tf_op jit(solution)/shard_map/ppermute | solution.py:17
  234.3 2.1 copy.18
  236.4 11.5 %collective-permute-done.1 = bf16[1024,256]{0,1:T(8,128)(2,1)} collective-permute-done((bf16[1024,256]{0,1:T(8,128)(2,1)}, bf16[1024,256]{0,1:T(8,128)(2,1)}, u32[]{:S(2)}, u32[]{:S(2)}) %collective-permute-start.1) | collective-permute-done | bytes 524320 | tf_op jit(solution)/shard_map/ppermute | solution.py:17
  247.9 14.6 %fusion.4 = f32[2,128,1024]{2,1,0:T(8,128)} fusion(pred[1024,3072]{1,0:T(8,128)(4,1)} %fusion.3, bf16[1024,2,128]{0,2,1:T(8,128)(2,1)} %bitcast.55, bf16[1024,2,128]{0,2,1:T(8,128)(2,1)S(1)} %bitcast.54, bf16[1024,2,128]{0,2,1:T(8,128)(2,1)} %bitcast.3, bf16[1024,2,128]{0,2,1:T(8,128)(2,1)} %bitcast.2, bf16[1024,2,128]{2,0,1:T(8,128)(2,1)} %copy.20, ...), kind=kOutput, calls=%fused_computation.10 | convolution fusion | flops 3274702848 | bytes 7864320 | tf_op jit(solution)/shard_map/hqk,khd->qhd/dot_general | solution.py:111
  262.5 87.1 %all-gather.7.cloned.1.call-done = bf16[32768,1,256]{0,2,1:T(8,128)(2,1)} async-done(((bf16[1024,1,256]{0,2,1:T(8,128)(2,1)}), bf16[32768,1,256]{0,2,1:T(8,128)(2,1)}) %all-gather.7.cloned.1.call-update) | async-done | bytes 16777232 | tf_op jit(solution)/shard_map/all_gather | solution.py:116
  349.6 20.9 %fusion.19 = f32[2,128,128]{2,1,0:T(8,128)S(1)} fusion(bf16[32768,2,128]{0,2,1:T(8,128)(2,1)} %bitcast.59, bf16[128,2,128]{0,2,1:T(8,128)(2,1)S(1)} %bitcast.57, bf16[32768,2,128]{0,2,1:T(8,128)(2,1)} %bitcast.60, pred[128,32768]{1,0:T(8,128)(4,1)} %fusion.1), kind=kOutput, calls=%fused_computation.24 | convolution fusion | flops 4353687552 | bytes 37945344 | tf_op jit(solution)/shard_map/hqk,khd->qhd/dot_general | solution.py:48
  370.6 0.9 fusion.42
  371.4 1.4 fusion.36
  372.8 9.5 %all-reduce = (f32[1152]{0:T(1024)S(1)}, f32[1152]{0:T(1024)S(1)}) all-reduce(f32[1152]{0:T(1024)S(1)} %get-tuple-element.3, f32[1152]{0:T(1024)S(1)} %get-tuple-element.2), channel_id=1, replica_groups=mesh['ctx'=32,'cand'=4] {'cand'}, use_global_device_ids=true, to_apply=%region_6.7 | all-reduce | flops 2304 | bytes 18432 | tf_op jit(solution)/shard_map/psum | solution.py:144
  382.3 4.5 %fusion.37 = f32[1152,1024]{1,0:T(8,128)} fusion(bf16[256,1024]{1,0:T(8,128)(2,1)S(1)} %copy-done, f32[128,256]{0,1:T(8,128)S(1)} %fusion.42, f32[1024,256]{0,1:T(8,128)} %bitcast.47, bf16[1152,4,256]{0,2,1:T(8,128)(2,1)} %bitcast.51, f32[256]{0:T(256)S(1)} %copy-done.8, f32[1152]{0:T(1024)S(1)} %get-tuple-element.14, f32[1152]{0:T(1024)S(1)} %get-tuple-element.13), kind=kOutput, calls=%fused_computation.41 | convolution fusion | flops 606044160 | bytes 7022592 | tf_op jit(solution)/shard_map/dot_general | solution.py:156
  386.8 49.2 %reduce-scatter.2.cloned.1.call-done = f32[1152,256]{1,0:T(8,128)} async-done(((f32[1152,1024]{1,0:T(8,128)}), f32[1152,256]{1,0:T(8,128)}) %reduce-scatter.2.cloned.1.call-update) | async-done | bytes 1179664 | tf_op jit(solution)/shard_map/reduce_scatter | solution.py:157
  436.0 1.5 add_convert_fusion
  437.5 0.8 slice.43
  (45 shorter events, 1.9 us)
Async XLA Ops:
  7.2 375.1 %copy-start = (bf16[256,1024]{1,0:T(8,128)(2,1)S(1)}, bf16[256,1024]{1,0:T(8,128)(2,1)}, u32[]{:S(2)}) copy-start(bf16[256,1024]{1,0:T(8,128)(2,1)} %param.19) | copy-start | bytes 1572868
  7.2 2.0 copy-start.5
  7.2 255.3 %all-gather.5.cloned.1.call-start = ((), (), s32[]{:S(2)}) async-start(), calls=%async_computation.2 | async-start | bytes 17301504 | tf_op jit(solution)/shard_map/all_gather | solution.py:117
  7.2 3.1 copy-start.3
  9.2 1.7 copy-start.11
  14.5 1.4 copy-start.2
  14.5 11.7 %copy-start.6 = (s32[1024]{0:T(1024)S(1)}, s32[1024]{0:T(1024)}, u32[]{:S(2)}) copy-start(s32[1024]{0:T(1024)} %param.12) | copy-start | bytes 12292
  14.5 112.8 %copy-start.7 = (s32[1024]{0:T(1024)S(1)}, s32[1024]{0:T(1024)}, u32[]{:S(2)}) copy-start(s32[1024]{0:T(1024)} %param.13) | copy-start | bytes 12292
  14.6 189.2 %copy-start.9 = (s32[128]{0:T(128)S(1)}, s32[128]{0:T(128)}, u32[]{:S(2)}) copy-start(s32[128]{0:T(128)} %param.15) | copy-start | bytes 1540
  14.6 189.2 %copy-start.10 = (s32[128]{0:T(128)S(1)}, s32[128]{0:T(128)}, u32[]{:S(2)}) copy-start(s32[128]{0:T(128)} %param.14) | copy-start | bytes 1540
  17.6 196.3 %copy-start.1 = (bf16[1024,1,256]{0,2,1:T(8,128)(2,1)S(1)}, bf16[1024,1,256]{0,2,1:T(8,128)(2,1)}, u32[]{:S(2)}) copy-start(bf16[1024,1,256]{0,2,1:T(8,128)(2,1)} %get-tuple-element.8) | copy-start | bytes 1572868
  17.6 332.0 %all-gather.7.cloned.1.call-start = ((), (), s32[]{:S(2)}) async-start(), calls=%async_computation.3 | async-start | bytes 17301504 | tf_op jit(solution)/shard_map/all_gather | solution.py:116
  18.3 417.6 %reduce-scatter.2.cloned.1.call-start = ((), (), s32[]{:S(2)}) async-start(), calls=%async_computation.1 | async-start | bytes 5898240 | tf_op jit(solution)/shard_map/reduce_scatter | solution.py:157
  18.4 196.5 %collective-permute-start.4 = (bf16[1024,256]{0,1:T(8,128)(2,1)}, bf16[1024,256]{0,1:T(8,128)(2,1)}, u32[]{:S(2)}, u32[]{:S(2)}) collective-permute-start(bf16[1024,256]{0,1:T(8,128)(2,1)} %get-tuple-element.6), channel_id=1, source_target_pairs={{0,4},{4,8},{8,12},{12,16},{16,20},{20,24},{24,28},{28,32},{32,36}... | collective-permute-start | bytes 1572872 | tf_op jit(solution)/shard_map/ppermute | solution.py:17
  23.2 196.0 %collective-permute-start = (bf16[1024,256]{0,1:T(8,128)(2,1)}, bf16[1024,256]{0,1:T(8,128)(2,1)}, u32[]{:S(2)}, u32[]{:S(2)}) collective-permute-start(bf16[1024,256]{0,1:T(8,128)(2,1)} %get-tuple-element.7), channel_id=1, source_target_pairs={{0,4},{4,8},{8,12},{12,16},{16,20},{20,24},{24,28},{28,32},{32,36}... | collective-permute-start | bytes 1572872 | tf_op jit(solution)/shard_map/ppermute | solution.py:17
  26.3 184.1 %collective-permute-start.2 = (s32[1024]{0:T(1024)S(1)}, s32[1024]{0:T(1024)S(1)}, u32[]{:S(2)}, u32[]{:S(2)}) collective-permute-start(s32[1024]{0:T(1024)S(1)} %copy-done.6), channel_id=1, source_target_pairs={{0,4},{4,8},{8,12},{12,16},{16,20},{20,24},{24,28},{28,32},{32,36}... | collective-permute-start | bytes 12296 | tf_op jit(solution)/shard_map/ppermute | solution.py:17
  210.4 4.5 %collective-permute-start.3 = (s32[1024]{0:T(1024)S(1)}, s32[1024]{0:T(1024)S(1)}, u32[]{:S(2)}, u32[]{:S(2)}) collective-permute-start(s32[1024]{0:T(1024)S(1)} %collective-permute-done.2), channel_id=1, source_target_pairs={{0,4},{4,8},{8,12},{12,16},{16,20},{20,24},{24,28},{28,32},{32,36}... | collective-permute-start | bytes 12296 | tf_op jit(solution)/shard_map/ppermute | solution.py:17
  214.9 33.0 %copy-start.4 = (bf16[1024,1,256]{0,2,1:T(8,128)(2,1)S(1)}, bf16[1024,1,256]{0,2,1:T(8,128)(2,1)}, u32[]{:S(2)}) copy-start(bf16[1024,1,256]{0,2,1:T(8,128)(2,1)} %get-tuple-element.10) | copy-start | bytes 1572868
  214.9 19.4 %collective-permute-start.5 = (bf16[1024,256]{0,1:T(8,128)(2,1)}, bf16[1024,256]{0,1:T(8,128)(2,1)}, u32[]{:S(2)}, u32[]{:S(2)}) collective-permute-start(bf16[1024,256]{0,1:T(8,128)(2,1)} %collective-permute-done.4), channel_id=1, source_target_pairs={{0,4},{4,8},{8,12},{12,16},{16,20},{20,24},{24,28},{28,32},{32,36}... | collective-permute-start | bytes 1572872 | tf_op jit(solution)/shard_map/ppermute | solution.py:17
  219.1 28.7 %collective-permute-start.1 = (bf16[1024,256]{0,1:T(8,128)(2,1)}, bf16[1024,256]{0,1:T(8,128)(2,1)}, u32[]{:S(2)}, u32[]{:S(2)}) collective-permute-start(bf16[1024,256]{0,1:T(8,128)(2,1)} %collective-permute-done), channel_id=1, source_target_pairs={{0,4},{4,8},{8,12},{12,16},{16,20},{20,24},{24,28},{28,32},{32,36}... | collective-permute-start | bytes 1572872 | tf_op jit(solution)/shard_map/ppermute | solution.py:17
  349.6 32.7 %copy-start.8 = (f32[256]{0:T(256)S(1)}, f32[256]{0:T(256)}, u32[]{:S(2)}) copy-start(f32[256]{0:T(256)} %param.18) | copy-start | bytes 3076
Sparse Core Ops, SparseCore 0:
  17.7 167.2 all-gather.4
  188.1 161.5 all-gather.6
  386.9 49.0 reduce-scatter.1
where the time goes:
time: 446 us; the launch traced here: 445 us
  blocking collectives  184 us (41%)
  waiting for transfers between devices  155 us (35%)
  matrix products  43.6 us (10%)
  starting transfers between devices  19.8 us (4%)
  other arithmetic  16.2 us (4%)
  between operations  14 us (3%)
  local copies, waits for them, and re-layouts  12.9 us (3%)
    all_gather x1, blocking collectives, shards(): lax.all_gather(history_valid, 'ctx', axis=0, tiled=True)  99 us
    all_gather x1, waiting for transfers between devices, shards(): lax.all_gather(hist_keys, 'ctx', axis=0, tiled=True)  87.1 us
    all_gather x1, blocking collectives, shards(): lax.all_gather(history_surface, 'ctx', axis=0, tiled=True)  75.5 us
    reduce_scatter x1, waiting for transfers between devices, shards(): shares = lax.psum_scatter(mixed, 'cand', scatter_dimension=1, tiled=True)  49.2 us
    dot_general x1, matrix products, cand_block(): jnp.einsum('hqk,khd->qhd', weights, split_heads(val_rows), preferred_elem...  20.9 us
    ppermute x6, starting transfers between devices, from_behind(): return lax.ppermute(block, axis, route)  19.7 us
    ppermute x6, waiting for transfers between devices, from_behind(): return lax.ppermute(block, axis, route)  17.9 us
    dot_general x1, matrix products, shards(): jnp.einsum('hqk,khd->qhd', weights, split_heads(window_vals), preferred_e...  14.6 us
  transfers between devices with their start and end apart: 9, of which 4 were waited for; matrix products, arithmetic and copies ran while one was open for 7% of the time, Pallas kernels for 0%

commit v1 on v0

--- a/solution.py
+++ b/solution.py
@@ -28,11 +28,10 @@
     return matrix.reshape(matrix.shape[0], matrix.shape[1] // HEAD, HEAD)
 
 
-def cand_block(queries, cutoff, surface, key_rows, val_rows, okay, key_surface, position):
+def cand_block(queries, cutoff, surface, key_rows, val_rows, key_surface, position):
     scale = 1.0 / math.sqrt(HEAD)
     mask = (
-        (okay[None, :] == 1)
-        & (position[None, :] < cutoff[:, None])
+        (position[None, :] < cutoff[:, None])
         & (key_surface[None, :] == surface[:, None])
     )
     scores = (
@@ -81,22 +80,28 @@
     cand_vals = proj[hist_rows:, 1]
     cand_query = proj[hist_rows:, 2]
     cand_keys = proj[hist_rows:, 3]
-    moving = (hist_keys, hist_vals, history_valid)
-    passed = []
-    for repeat in range(2):
-        moving = from_behind((moving[0], moving[1], moving[2]), "ctx", 1)
-        passed.append(moving)
-    second_back = passed[1]
-    first_back = passed[0]
-    window_keys = jnp.concatenate([second_back[0], first_back[0], hist_keys], 0)
-    window_vals = jnp.concatenate([second_back[1], first_back[1], hist_vals], 0)
-    window_okay = jnp.concatenate([second_back[2], first_back[2], history_valid], 0)
+    hist_vals = jnp.where(history_valid[:, None] == 1, hist_vals, 0).astype(jnp.bfloat16)
+    both = jnp.concatenate([hist_keys, hist_vals], 1)
+    first_back = from_behind(both, "ctx", 1)
+    second_back = from_behind(both, "ctx", 2)
+    window_keys = jnp.concatenate(
+        [second_back[:, :local_width], first_back[:, :local_width], hist_keys], 0
+    )
+    window_vals = jnp.concatenate(
+        [second_back[:, local_width:], first_back[:, local_width:], hist_vals], 0
+    )
+    limits = jnp.concatenate(
+        [candidate_cutoff // 256, candidate_cutoff % 256, candidate_surface, candidate_surface]
+    )
+    limits = jnp.zeros((16, local_width), jnp.bfloat16).at[:2].set(
+        limits.reshape(2, local_width).astype(jnp.bfloat16)
+    )
+    asked = lax.all_gather(jnp.concatenate([cand_query, limits], 0), "ctx", axis=0)
     row_idx = jnp.arange(hist_rows, dtype=jnp.int32)
     col_idx = jnp.arange(3 * hist_rows, dtype=jnp.int32)
     window_mask = (
         (col_idx[None, :] > row_idx[:, None])
         & (col_idx[None, :] <= row_idx[:, None] + 2 * hist_rows)
-        & (window_okay[None, :] == 1)
     )
     scores = (
         jnp.einsum(
@@ -112,23 +117,21 @@
         "hqk,khd->qhd", weights, split_heads(window_vals), preferred_element_type=jnp.float32
     )
     hist_attn = hist_attn.reshape(hist_rows, local_width)
-    piece = (
-        lax.all_gather(hist_keys, "ctx", axis=0, tiled=True),
-        lax.all_gather(hist_vals, "ctx", axis=0, tiled=True),
-        lax.all_gather(history_valid, "ctx", axis=0, tiled=True),
-        lax.all_gather(history_surface, "ctx", axis=0, tiled=True),
-    )
-    position = jnp.arange(piece[0].shape[0], dtype=jnp.int32)
-    cand_attn = cand_block(
-        cand_query,
-        candidate_cutoff,
-        candidate_surface,
-        piece[0],
-        piece[1],
-        piece[2],
-        piece[3],
+    every_query = asked[:, :cand_rows].reshape(-1, local_width)
+    told = asked[:, cand_rows : cand_rows + 2].astype(jnp.int32)
+    every_cutoff = (told[:, 0, :cand_rows] * 256 + told[:, 0, cand_rows:]).reshape(-1)
+    every_surface = told[:, 1, :cand_rows].reshape(-1)
+    position = lax.axis_index("ctx") * hist_rows + jnp.arange(hist_rows, dtype=jnp.int32)
+    partial = cand_block(
+        every_query,
+        every_cutoff,
+        every_surface,
+        hist_keys,
+        hist_vals,
+        history_surface,
         position,
     )
+    cand_attn = lax.psum_scatter(partial, "ctx", scatter_dimension=0, tiled=True)
     self_score = (
         jnp.sum(
             split_heads(cand_query).astype(jnp.float32)

time: 446 us -> 406 us (0.910)
  blocking collectives: 184 us -> 31.1 us
  waiting for transfers between devices: 155 us -> 260 us
  local copies, waits for them, and re-layouts: 12.9 us -> 27.1 us
  starting transfers between devices: 19.8 us -> 8.4 us
  other arithmetic: 16.2 us -> 22.4 us
    all_gather x2 -> x0, blocking collectives: 175 us -> none  [the longest x1 99 us: shards(): lax.all_gather(history_valid, 'ctx', axis=0, tiled=True)]
    reduce_scatter x0 -> x1, waiting for transfers between devices: none -> 101 us  [shards(): lax.psum_scatter(partial, 'ctx', scatter_dimension=0, tiled=True)]
    psum x1, blocking collectives: 9.46 us -> 31.1 us  [shards(): lax.psum((jnp.sum(attn, axis=-1), jnp.sum(attn * attn, axis=-1)), 'cand')]
    ppermute x6 -> x2, waiting for transfers between devices: 17.9 us -> 38.4 us  [from_behind(): return lax.ppermute(block, axis, route)]
    all_gather x2 -> x1, waiting for transfers between devices: 87.1 us -> 70.7 us  [shards(): lax.all_gather(jnp.concatenate([cand_query, limits], 0), 'ctx', axis=0)]
    ppermute x6 -> x2, starting transfers between devices: 19.7 us -> 8.1 us  [from_behind(): return lax.ppermute(block, axis, route)]
    slice x1 -> x4, local copies, waits for them, and re-layouts: 0.88 us -> 10.3 us  [the longest x1 3.12 us: shards(): every_query = asked[:, :cand_rows].reshape(-1, local_width)]
    concatenate x0 -> x4, other arithmetic: none -> 4.61 us  [the longest x1 2.45 us: shards(): jnp.concatenate([second_back[:, local_width:], first_back[:, local_width:...]
  transfers between devices with their start and end apart: 9 -> 5, of which waited for: 4 -> 5; matrix products, arithmetic and copies ran while one was open for 7% -> 10% of each run, Pallas kernels for 0% -> 0%
where the time goes in v1:
time: 406 us; the launch traced here: 405 us
  waiting for transfers between devices  260 us (64%)
  matrix products  42.6 us (10%)
  blocking collectives  31.1 us (8%)
  local copies, waits for them, and re-layouts  27.1 us (7%)
  other arithmetic  22.4 us (6%)
  between operations  14 us (3%)
  starting transfers between devices  8.4 us (2%)
    reduce_scatter x1, waiting for transfers between devices, shards(): lax.psum_scatter(partial, 'ctx', scatter_dimension=0, tiled=True)  101 us
    all_gather x1, waiting for transfers between devices, shards(): lax.all_gather(jnp.concatenate([cand_query, limits], 0), 'ctx', axis=0)  70.7 us
    reduce_scatter x1, waiting for transfers between devices, shards(): shares = lax.psum_scatter(mixed, 'cand', scatter_dimension=1, tiled=True)  49.4 us
    ppermute x2, waiting for transfers between devices, from_behind(): return lax.ppermute(block, axis, route)  38.4 us
    psum x1, blocking collectives, shards(): lax.psum((jnp.sum(attn, axis=-1), jnp.sum(attn * attn, axis=-1)), 'cand')  31.1 us
    dot_general x1, matrix products, cand_block(): jnp.einsum('hqk,khd->qhd', weights, split_heads(val_rows), preferred_elem...  19.9 us
    dot_general x1, matrix products, shards(): jnp.einsum('hqk,khd->qhd', weights, split_heads(window_vals), preferred_e...  14.7 us
  transfers between devices with their start and end apart: 5, of which 5 were waited for; matrix products, arithmetic and copies ran while one was open for 10% of the time, Pallas kernels for 0%

profile of v1, /device:TPU:1, one launch (start us, length us, event | category | flops | bytes accessed | tf_op | source)
XLA Modules:
  0.0 405.4 jit_solution(4874344462393631874)
XLA Ops:
  7.2 1.8 constant_dynamic-update-slice_fusion.1
  11.2 3.6 multiply_convert_fusion
  14.9 1.5 copy-done.1
  17.6 2.6 fusion.58
  20.2 70.7 %all-gather.3.cloned.1.call-done = bf16[4608,256]{1,0:T(8,128)(2,1)} async-done(((bf16[144,256]{1,0:T(8,128)(2,1)}), bf16[4608,256]{1,0:T(8,128)(2,1)}) %all-gather.3.cloned.1.call-update) | async-done | bytes 2359312 | tf_op jit(solution)/shard_map/all_gather | solution.py:99
  91.0 0.9 slice_convert_fusion
  91.9 3.1 slice.100
  95.0 4.0 reshape.220
  99.1 5.5 %compare_and_fusion = pred[4096,1024]{1,0:T(8,128)(4,1)} fusion(s32[1024]{0:T(1024)S(1)} %copy-done.6, s32[1024]{0:T(1024)S(1)} %iota_add_fusion, s32[4096]{0:T(1024)S(1)} %bitcast.65, s32[4096]{0:T(1024)S(1)} %bitcast.64), kind=kLoop, calls=%fused_computation.2 | loop fusion | flops 12582912 | bytes 4235264 | tf_op jit(solution)/shard_map/and | solution.py:34
  104.6 19.9 %fusion = f32[2,128,4096]{2,1,0:T(8,128)} fusion(pred[4096,1024]{1,0:T(8,128)(4,1)} %compare_and_fusion, bf16[1024,2,128]{0,2,1:T(8,128)(2,1)S(1)} %bitcast.52, bf16[4096,2,128]{2,1,0:T(2,128)(2,1)} %reshape.220, bf16[1024,2,128]{0,2,1:T(8,128)(2,1)} %bitcast.62, pred[1024]{0:T(1024)(128)(4,1)S(1)} %broadcast_compare_fusion), kind=kOutput, calls=%fused_computation.3 | convolution fusion | flops 4353949696 | bytes 11535360 | tf_op jit(solution)/shard_map/hqk,khd->qhd/dot_general | solution.py:47
  124.5 1.1 bitcast_select_fusion
  125.6 2.1 pad_maximum_fusion.2
  127.7 4.9 %collective-permute-start = (bf16[1024,512]{0,1:T(8,128)(2,1)}, bf16[1024,512]{0,1:T(8,128)(2,1)}, u32[]{:S(2)}, u32[]{:S(2)}) collective-permute-start(bf16[1024,512]{0,1:T(8,128)(2,1)} %pad_maximum_fusion.2), channel_id=1, source_target_pairs={{0,8},{4,12},{8,16},{12,20},{16,24},{20,28},{24,32},{28,36},{32,40... | collective-permute-start | bytes 3145736 | tf_op jit(solution)/shard_map/ppermute | solution.py:17
  132.6 3.2 collective-permute-start.1
  135.8 2.1 copy.23
  137.9 0.9 convert_multiply_fusion.2
  138.9 4.3 %fusion.3 = pred[1024,3072]{1,0:T(8,128)(4,1)} fusion(s32[1024]{0:T(1024)S(1)} %iota_add_fusion.1), kind=kLoop, calls=%fused_computation.7 | loop fusion | flops 9437184 | bytes 3149824 | tf_op jit(solution)/shard_map/and | solution.py:103
  143.1 13.9 %collective-permute-done = bf16[1024,512]{0,1:T(8,128)(2,1)} collective-permute-done((bf16[1024,512]{0,1:T(8,128)(2,1)}, bf16[1024,512]{0,1:T(8,128)(2,1)}, u32[]{:S(2)}, u32[]{:S(2)}) %collective-permute-start) | collective-permute-done | bytes 1048608 | tf_op jit(solution)/shard_map/ppermute | solution.py:17
  157.0 2.2 fusion.59
  159.3 2.1 copy.21
  161.4 24.5 %collective-permute-done.1 = bf16[1024,512]{0,1:T(8,128)(2,1)} collective-permute-done((bf16[1024,512]{0,1:T(8,128)(2,1)}, bf16[1024,512]{0,1:T(8,128)(2,1)}, u32[]{:S(2)}, u32[]{:S(2)}) %collective-permute-start.1) | collective-permute-done | bytes 1048608 | tf_op jit(solution)/shard_map/ppermute | solution.py:17
  185.8 2.3 fusion.60
  188.1 2.1 copy.22
  190.2 2.4 pad_maximum_fusion
  192.6 14.7 %fusion.4 = f32[2,128,1024]{2,1,0:T(8,128)} fusion(bf16[3072,2,128]{0,2,1:T(8,128)(2,1)} %bitcast.60, pred[1024,3072]{1,0:T(8,128)(4,1)} %fusion.3, bf16[1024,2,128]{0,2,1:T(8,128)(2,1)} %bitcast.61, bf16[1024,2,128]{2,0,1:T(8,128)(2,1)} %copy.23, bf16[1024,2,128]{2,0,1:T(8,128)(2,1)} %copy.22, bf16[1024,2,128]{2,0,1:T(8,128)(2,1)} %copy.21), kind=kOutput, calls=%fused_computation.8 | convolution fusion | flops 3269984256 | bytes 7864320 | tf_op jit(solution)/shard_map/hqk,khd->qhd/dot_general | solution.py:116
  207.3 101.3 %reduce-scatter.3.cloned.1.call-done = f32[128,256]{0,1:T(8,128)} async-done(((f32[4096,256]{0,1:T(8,128)}), f32[128,256]{0,1:T(8,128)}) %reduce-scatter.3.cloned.1.call-update) | async-done | bytes 131088 | tf_op jit(solution)/shard_map/reduce_scatter | solution.py:134
  308.6 0.9 fusion.43
  309.5 1.4 fusion.32
  310.9 31.1 %all-reduce.1 = (f32[1152]{0:T(1024)S(1)}, f32[1152]{0:T(1024)S(1)}) all-reduce(f32[1152]{0:T(1024)S(1)} %get-tuple-element.15, f32[1152]{0:T(1024)S(1)} %get-tuple-element.14), channel_id=1, replica_groups=mesh['ctx'=32,'cand'=4] {'cand'}, use_global_device_ids=true, to_apply=%region_7.8 | all-reduce | flops 2304 | bytes 18432 | tf_op jit(solution)/shard_map/psum | solution.py:147
  342.0 4.4 %fusion.33 = f32[1152,1024]{1,0:T(8,128)} fusion(bf16[256,1024]{1,0:T(8,128)(2,1)S(1)} %copy-done, f32[128,256]{0,1:T(8,128)S(1)} %fusion.43, f32[1024,256]{0,1:T(8,128)} %bitcast.45, bf16[1152,4,256]{0,2,1:T(8,128)(2,1)} %bitcast.51, f32[256]{0:T(256)S(1)} %copy-done.7, f32[1152]{0:T(1024)S(1)} %get-tuple-element.29, f32[1152]{0:T(1024)S(1)} %get-tuple-element.28), kind=kOutput, calls=%fused_computation.36 | convolution fusion | flops 606044160 | bytes 7022592 | tf_op jit(solution)/shard_map/dot_general | solution.py:159
  346.5 49.4 %reduce-scatter.5.cloned.1.call-done = f32[1152,256]{1,0:T(8,128)} async-done(((f32[1152,1024]{1,0:T(8,128)}), f32[1152,256]{1,0:T(8,128)}) %reduce-scatter.5.cloned.1.call-update) | async-done | bytes 1179664 | tf_op jit(solution)/shard_map/reduce_scatter | solution.py:160
  395.9 1.5 add_convert_fusion
  (50 shorter events, 5.0 us)
Async XLA Ops:
  7.2 334.8 %copy-start = (bf16[256,1024]{1,0:T(8,128)(2,1)S(1)}, bf16[256,1024]{1,0:T(8,128)(2,1)}, u32[]{:S(2)}) copy-start(bf16[256,1024]{1,0:T(8,128)(2,1)} %param.21) | copy-start | bytes 1572868
  7.2 1.9 copy-start.4
  7.2 83.8 %all-gather.3.cloned.1.call-start = ((), (), s32[]{:S(2)}) async-start(), calls=%async_computation.4 | async-start | bytes 2433024 | tf_op jit(solution)/shard_map/all_gather | solution.py:99
  9.1 1.6 copy-start.3
  9.5 1.7 copy-start.8
  11.2 5.1 %copy-start.9 = (s32[128]{0:T(128)S(1)}, s32[128]{0:T(128)}, u32[]{:S(2)}) copy-start(s32[128]{0:T(128)} %param.17) | copy-start | bytes 1540
  11.2 5.2 %copy-start.10 = (s32[128]{0:T(128)S(1)}, s32[128]{0:T(128)}, u32[]{:S(2)}) copy-start(s32[128]{0:T(128)} %param.16) | copy-start | bytes 1540
  11.2 6.4 %copy-start.5 = (s32[1024]{0:T(1024)S(1)}, s32[1024]{0:T(1024)}, u32[]{:S(2)}) copy-start(s32[1024]{0:T(1024)} %param.14) | copy-start | bytes 12292
  14.9 1.5 copy-start.1
  17.3 291.3 %reduce-scatter.3.cloned.1.call-start = ((), (), s32[]{:S(2)}) async-start(), calls=%async_computation.2 | async-start | bytes 4325376 | tf_op jit(solution)/shard_map/reduce_scatter | solution.py:134
  20.2 84.3 %copy-start.2 = (bf16[1024,1,256]{0,2,1:T(8,128)(2,1)}, bf16[1024,1,256]{0,2,1:T(8,128)(2,1)S(1)}, u32[]{:S(2)}) copy-start(bf16[1024,1,256]{0,2,1:T(8,128)(2,1)S(1)} %get-tuple-element.21) | copy-start | bytes 1572868
  95.0 4.0 copy-start.6
  124.4 271.4 %reduce-scatter.5.cloned.1.call-start = ((), (), s32[]{:S(2)}) async-start(), calls=%async_computation.3 | async-start | bytes 5898240 | tf_op jit(solution)/shard_map/reduce_scatter | solution.py:160
  127.7 29.3 %collective-permute-start = (bf16[1024,512]{0,1:T(8,128)(2,1)}, bf16[1024,512]{0,1:T(8,128)(2,1)}, u32[]{:S(2)}, u32[]{:S(2)}) collective-permute-start(bf16[1024,512]{0,1:T(8,128)(2,1)} %pad_maximum_fusion.2), channel_id=1, source_target_pairs={{0,8},{4,12},{8,16},{12,20},{16,24},{20,28},{24,32},{28,36},{32,40... | collective-permute-start | bytes 3145736 | tf_op jit(solution)/shard_map/ppermute | solution.py:17
  132.6 53.2 %collective-permute-start.1 = (bf16[1024,512]{0,1:T(8,128)(2,1)}, bf16[1024,512]{0,1:T(8,128)(2,1)}, u32[]{:S(2)}, u32[]{:S(2)}) collective-permute-start(bf16[1024,512]{0,1:T(8,128)(2,1)} %pad_maximum_fusion.2), channel_id=1, source_target_pairs={{0,4},{4,8},{8,12},{12,16},{16,20},{20,24},{24,28},{28,32},{32,36}... | collective-permute-start | bytes 3145736 | tf_op jit(solution)/shard_map/ppermute | solution.py:17
  192.6 149.4 %copy-start.7 = (f32[256]{0:T(256)S(1)}, f32[256]{0:T(256)}, u32[]{:S(2)}) copy-start(f32[256]{0:T(256)} %param.20) | copy-start | bytes 3076
Sparse Core Ops, SparseCore 0:
  17.5 73.4 all-gather.2
  124.6 183.9 reduce-scatter.2
  346.6 49.2 reduce-scatter.4

commit v2 on v0

v2 whole, which is shorter than its diff:
```python
import functools
import math

import jax
import jax.numpy as jnp
from jax import lax
from jax.experimental import pallas as pl
from jax.experimental.pallas import tpu as pltpu
from jax.sharding import PartitionSpec as P

HEAD = 128
EPS = 1e-05
HALF_SCALE = 0.5 / math.sqrt(HEAD)
FAR = 2.0**60
CHUNK = 256
CARDS = 128
META = 16
BF16 = jnp.bfloat16
F32 = jnp.float32
MESH = pl.DeviceIdType.MESH
NT = (((1,), (1,)), ((), ()))

S_W, S_QY, S_QX, S_QZ = 0, 3, 4, 7
S_H1, S_H2 = 10, 14
S_PZ, S_PX, S_PY = 18, 21, 24
S_ST, S_G = 25, 40
N_SEM = 55


def silu_of_half(half):
    return half * jnp.tanh(half) + half


def kernel(
    x_ref, cx_ref, valid_ref, hsurf_ref, csurf_ref, ccut_ref, gin_ref, w_ref, gout_ref, wo_ref,
    oh_ref, oc_ref,
    kv, hkv, qh, uh, cp, kf, vt, qall, qf, lcb, own, pz, rz, px, rx, py, ry, attn, cattn, st, gf, wc,
    ssem, rsem,
):
    c = lax.axis_index("ctx")
    h = lax.axis_index("cand")
    yh, z, xx = c // 16, (c // 4) % 4, c % 4

    def at_x(d):
        return (yh * 16 + z * 4 + (xx + d + 4) % 4, h)

    def at_z(d):
        return (yh * 16 + ((z + d + 4) % 4) * 4 + xx, h)

    def at_y():
        return ((c + 16) % 32, h)

    def at_c(d):
        return ((c + d + 32) % 32, h)

    def at_h(d):
        return (c, (h + d) % 4)

    core_peer = (c, h + 1 - 2 * (h % 2))
    y_peer = (c, (h + 2) % 4)

    barrier = pltpu.get_barrier_semaphore()
    greeted = [at_h(1), at_h(2), at_h(3), at_y(), at_x(1), at_x(2), at_x(3), at_z(1), at_z(2), at_z(3)]
    greeted += [at_c(1), at_c(2), at_c(-1), at_c(-2)]
    for device in greeted:
        pl.semaphore_signal(barrier, inc=1, device_id=device, device_id_type=MESH)

    def remote(src, dst, slot, device):
        return pltpu.make_async_remote_copy(
            src_ref=src, dst_ref=dst, send_sem=ssem.at[slot], recv_sem=rsem.at[slot],
            device_id=device, device_id_type=MESH,
        )

    sent = []

    def send(*args):
        copy = remote(*args)
        copy.start()
        sent.append(copy)
        return copy

    def project(rows):
        values = rows.astype(F32)
        center = values - jnp.mean(values, axis=-1, keepdims=True)
        spread = jnp.mean(center * center, axis=-1, keepdims=True)
        normed = (center * lax.rsqrt(spread + EPS) * gin_ref[...]).astype(BF16)
        half = jnp.dot(normed, w_ref[...], preferred_element_type=F32) * 0.5
        return silu_of_half(half).astype(BF16)

    cp[...] = project(cx_ref[...])
    qall[0, 0, 0, 0:CARDS, :] = cp[:, 512:768]
    cut = ccut_ref[...]
    limits = jnp.concatenate([lax.shift_right_logical(cut, 8), cut & 255], 1).astype(F32)
    surf = csurf_ref[...].astype(F32)
    surf = jnp.concatenate([surf, surf], 1)
    row = lax.broadcasted_iota(jnp.int32, (META, 256), 0)
    qall[0, 0, 0, CARDS:, :] = jnp.where(row == 0, limits, jnp.where(row == 1, surf, 0.0)).astype(BF16)

    pl.semaphore_wait(barrier, len(greeted))
    q_y = send(qall.at[0, 0, 0], qall.at[0, 0, 1], S_QY, at_y())

    vt[...] = jnp.transpose(valid_ref[...].astype(F32))
    surf_t = jnp.transpose(hsurf_ref[...].astype(F32))
    lane = lax.broadcasted_iota(jnp.int32, (CARDS, 128), 1).astype(F32)
    for i in range(8):
        kf[i * 128 : i * 128 + 128, :] = jnp.where(surf_t[:, i : i + 1] == lane, 1.0, 0.0).astype(BF16)

    def hist_chunk(i):
        at = slice(i * CHUNK, i * CHUNK + CHUNK)
        proj = project(x_ref[at, :])
        okay = jnp.concatenate([vt[:, 2 * i : 2 * i + 1], vt[:, 2 * i + 1 : 2 * i + 2]], 0)
        uh[at, :] = proj[:, 0:256]
        qh[at, :] = proj[:, 512:768]
        kv[at, 0:256] = proj[:, 768:1024]
        kv[at, 256:512] = (proj[:, 256:512].astype(F32) * okay).astype(BF16)
        return send(kv.at[at], hkv.at[0, at], S_H1 + i, at_c(1))

    first = [hist_chunk(0)]
    q_y.wait_recv()
    q_x = [None] + [send(qall.at[0, 0], qall.at[0, d], S_QX + d - 1, at_x(d)) for d in (1, 2, 3)]
    first.append(hist_chunk(1))
    first.append(hist_chunk(2))
    for d in (1, 2, 3):
        q_x[d].wait_recv()
    q_z = [None] + [send(qall.at[0], qall.at[d], S_QZ + d - 1, at_z(d)) for d in (1, 2, 3)]
    first.append(hist_chunk(3))
    second = [None] * 4
    for i in (3, 2, 1, 0):
        at = slice(i * CHUNK, i * CHUNK + CHUNK)
        second[i] = send(kv.at[at], hkv.at[1, at], S_H2 + i, at_c(2))
    mine = pl.ds(pl.multiple_of(h * 256, 256), 256)
    into = []
    for d in (1, 2, 3):
        theirs = pl.ds(pl.multiple_of(((h + d) % 4) * 256, 256), 256)
        into.append(send(wo_ref.at[:, theirs], wc.at[mine, :], S_W + d - 1, at_h(d)))
    wc[mine, :] = wo_ref[:, mine]

    def attend(queries, keys, values, mask):
        half = lax.dot_general(queries, keys, NT, preferred_element_type=F32) * HALF_SCALE
        weights = silu_of_half(half)
        if mask is not None:
            weights = jnp.where(mask(weights.shape), weights, 0.0)
        return jnp.dot(weights.astype(BF16), values, preferred_element_type=F32)

    def hist_tile(keys_ref, j, lo, hi, mask):
        ks = slice(j * CHUNK, j * CHUNK + CHUNK)
        out = []
        for head in range(2):
            a, b = head * 128, head * 128 + 128
            out.append(attend(qh[lo:hi, a:b], keys_ref[ks, a:b], keys_ref[ks, 256 + a : 256 + b], mask))
        return jnp.concatenate(out, 1)

    def not_later(shape):
        return lax.broadcasted_iota(jnp.int32, shape, 1) <= lax.broadcasted_iota(jnp.int32, shape, 0)

    attn[...] = hist_tile(kv, 0, 0, 1024, not_later)
    for j in (1, 2, 3):
        attn[j * CHUNK :, :] += hist_tile(kv, j, j * CHUNK, 1024, not_later)

    start = (c * 1024).astype(F32)

    def cand_plane(dz):
        for dx in range(4):
            for dy in range(2):
                told = qall[dz, dx, dy, CARDS:, :].astype(F32)
                local = told[0:8, 0:128] * 256.0 + told[0:8, 128:256] - start
                both = jnp.where(
                    lax.broadcasted_iota(jnp.int32, (8, 128), 0) == 0, local, told[0:8, 0:128]
                )
                both = jnp.transpose(both)
                r = (dx * 2 + dy) * 128
                lcb[r : r + 128, :] = jnp.broadcast_to(both[:, 0:1], (128, 128))
                qf[r : r + 128, :] = jnp.where(both[:, 1:2] == lane, 0.0, -FAR).astype(BF16)

        heads = []
        for head in range(2):
            a, b = head * 128, head * 128 + 128
            queries = jnp.concatenate(
                [qall[dz, dx, dy, 0:CARDS, a:b] for dx in range(4) for dy in range(2)], 0
            )
            queries = jnp.concatenate([queries, qf[...]], 1)
            total = None
            for j in range(4):
                ks = slice(j * CHUNK, j * CHUNK + CHUNK)
                keys = jnp.concatenate([kv[ks, a:b], kf[ks, :]], 1)

                def mask(shape):
                    place = (lax.broadcasted_iota(jnp.int32, shape, 1) + j * CHUNK).astype(F32)
                    return place < jnp.concatenate([lcb[...], lcb[...]], 1)

                part = attend(queries, keys, kv[ks, 256 + a : 256 + b], mask)
                total = part if total is None else total + part
            heads.append(total)
        return jnp.concatenate(heads, 1)

    own[...] = cand_plane(0)
    p_z = [None] * 4
    for d in (1, 3, 2):
        q_z[d].wait_recv()
        pz[d - 1] = cand_plane(d).astype(BF16)
        p_z[d] = send(pz.at[d - 1], rz.at[d - 1], S_PZ + d - 1, at_z(-d))

    for i in range(4):
        first[i].wait_recv()

    @pl.when(c >= 1)
    def _():
        for j in range(4):
            attn[...] += hist_tile(hkv.at[0], j, 0, 1024, None)

    for d in (1, 3, 2):
        p_z[d].wait_recv()
    total = own[...]
    for d in (1, 2, 3):
        total += rz[d - 1].astype(F32)
    px[...] = total.astype(BF16)
    p_x = [None] + [
        send(px.at[pl.ds(d * 256, 256)], rx.at[d - 1], S_PX + d - 1, at_x(-d)) for d in (1, 2, 3)
    ]
    own[0:256, :] = total[0:256]

    full = 1024.0

    def chunk_rows(i):
        return (slice(i * CHUNK, i * CHUNK + CHUNK), CHUNK) if i < 4 else (slice(1024, 1152), CARDS)

    def stats_out(i, values):
        size = values.shape[0]
        sums = jnp.sum(values, axis=-1, keepdims=True)
        squares = jnp.sum(values * values, axis=-1, keepdims=True)
        spread = lax.broadcasted_iota(jnp.int32, (size, 128), 1)
        st[0, i, :, 0:size] = jnp.transpose(jnp.where(spread == 0, sums, squares))[0:8, :]
        return [
            send(st.at[0, i], st.at[d, i], S_ST + 3 * i + d - 1, at_h(d)) for d in (1, 2, 3)
        ]

    def gate_out(i, values, update, got):
        at, size = chunk_rows(i)
        for copy in got:
            copy.wait_recv()
        both = (st[0, i] + st[1, i] + st[2, i] + st[3, i])[:, 0:size] / full
        both = jnp.transpose(both)
        mean, square = both[:, 0:1], both[:, 1:2]
        gated = (values - mean) * lax.rsqrt(square - mean * mean + EPS) * gout_ref[...] * update.astype(F32)
        gf[at, mine] = gated.astype(BF16)
        block = gf.at[at, mine]
        return [
            send(block, block, S_G + 3 * i, core_peer),
            send(block, block, S_G + 3 * i + 1, y_peer),
        ]

    across = pl.ds(pl.multiple_of(((h + 2) % 4) * 256, 256), 256)

    def gate_forward(i, moving):
        at, _ = chunk_rows(i)
        moving[1].wait_recv()
        block = gf.at[at, across]
        moving.append(send(block, block, S_G + 3 * i + 2, core_peer))

    def finish(i, moving, rows_ref, out_ref):
        at, size = chunk_rows(i)
        moving[0].wait_recv()
        moving[2].wait_recv()
        where = at if i < 4 else slice(0, CARDS)
        mixed = jnp.dot(gf[at, :], wc[...], preferred_element_type=F32)
        out_ref[where, :] = (rows_ref[where, mine].astype(F32) + mixed).astype(BF16)

    got, moving = {}, {}
    for copy in into:
        copy.wait_recv()
    for i in (3, 2, 1, 0):
        second[i].wait_recv()

        @pl.when(c >= 2)
        def _():
            def later(shape):
                return (
                    lax.broadcasted_iota(jnp.int32, shape, 1) + i * CHUNK
                    > lax.broadcasted_iota(jnp.int32, shape, 0)
                )

            hi = i * CHUNK + CHUNK
            attn[0:hi, :] += hist_tile(hkv.at[1], i, 0, hi, later)

        at, _size = chunk_rows(i)
        got[i] = stats_out(i, attn[at, :])
        if i == 3:
            for d in (1, 2, 3):
                p_x[d].wait_recv()
            total = own[0:256, :]
            for d in (1, 2, 3):
                total += rx[d - 1].astype(F32)
            own[0:CARDS, :] = total[0:CARDS]
            py[...] = total[CARDS:]
            p_y = send(py, ry, S_PY, at_y())
        if i == 2:
            p_y.wait_recv()
            total = own[0:CARDS, :] + ry[...]
            selfs = []
            for head in range(2):
                a, b = head * 128, head * 128 + 128
                query = cp[:, 512 + a : 512 + b].astype(F32)
                key = cp[:, 768 + a : 768 + b].astype(F32)
                half = jnp.sum(query * key, axis=-1, keepdims=True) * HALF_SCALE
                weight = silu_of_half(half).astype(BF16).astype(F32)
                selfs.append(weight * cp[:, 256 + a : 256 + b].astype(F32))
            cattn[...] = total + jnp.concatenate(selfs, 1)
            got[4] = stats_out(4, cattn[...])
        if i <= 2:
            k = i + 1
            where = chunk_rows(k)[0]
            moving[k] = gate_out(k, attn[where, :], uh[where, :], got[k])
        if i == 1:
            moving[4] = gate_out(4, cattn[...], cp[:, 0:256], got[4])
            gate_forward(3, moving[3])
        if i == 0:
            gate_forward(2, moving[2])
            gate_forward(4, moving[4])
    moving[0] = gate_out(0, attn[0:CHUNK, :], uh[0:CHUNK, :], got[0])
    finish(3, moving[3], x_ref, oh_ref)
    gate_forward(1, moving[1])
    finish(2, moving[2], x_ref, oh_ref)
    finish(4, moving[4], cx_ref, oc_ref)
    gate_forward(0, moving[0])
    finish(1, moving[1], x_ref, oh_ref)
    finish(0, moving[0], x_ref, oh_ref)
    for copy in sent:
        copy.wait_send()


def shards(
    history,
    candidates,
    history_valid,
    history_surface,
    candidate_surface,
    candidate_cutoff,
    gain_in,
    w_uvqk,
    gain_out,
    w_out,
):
    vmem = pl.BlockSpec(memory_space=pltpu.VMEM)
    return pl.pallas_call(
        kernel,
        out_shape=(
            jax.ShapeDtypeStruct((1024, 256), BF16),
            jax.ShapeDtypeStruct((CARDS, 256), BF16),
        ),
        in_specs=[vmem] * 10,
        out_specs=(vmem, vmem),
        scratch_shapes=[
            pltpu.VMEM((1024, 512), BF16),
            pltpu.VMEM((2, 1024, 512), BF16),
            pltpu.VMEM((1024, 256), BF16),
            pltpu.VMEM((1024, 256), BF16),
            pltpu.VMEM((CARDS, 1024), BF16),
            pltpu.VMEM((1024, 128), BF16),
            pltpu.VMEM((128, 8), F32),
            pltpu.VMEM((4, 4, 2, CARDS + META, 256), BF16),
            pltpu.VMEM((1024, 128), BF16),
            pltpu.VMEM((1024, 128), F32),
            pltpu.VMEM((1024, 256), F32),
            pltpu.VMEM((3, 1024, 256), BF16),
            pltpu.VMEM((3, 1024, 256), BF16),
            pltpu.VMEM((1024, 256), BF16),
            pltpu.VMEM((3, 256, 256), BF16),
            pltpu.VMEM((CARDS, 256), F32),
            pltpu.VMEM((CARDS, 256), F32),
            pltpu.VMEM((1024, 256), F32),
            pltpu.VMEM((CARDS, 256), F32),
            pltpu.VMEM((4, 5, 8, 256), F32),
            pltpu.VMEM((1152, 1024), BF16),
            pltpu.VMEM((1024, 256), BF16),
            pltpu.SemaphoreType.DMA((N_SEM,)),
            pltpu.SemaphoreType.DMA((N_SEM,)),
        ],
        compiler_params=pltpu.CompilerParams(
            collective_id=0, has_side_effects=True, vmem_limit_bytes=56 * 2**20
        ),
        name="hstu",
    )(
        history,
        candidates,
        history_valid.reshape(8, 128),
        history_surface.reshape(8, 128),
        candidate_surface.reshape(1, CARDS),
        candidate_cutoff.reshape(1, CARDS),
        gain_in.reshape(1, 1024),
        w_uvqk.reshape(1024, 1024),
        gain_out.reshape(1, 256),
        w_out,
    )


def solution(mesh):
    placed = (
        P("ctx", None),
        P("ctx", None),
        P("ctx"),
        P("ctx"),
        P("ctx"),
        P("ctx"),
        P(),
        P(None, None, "cand"),
        P("cand"),
        P("cand", None),
    )
    return jax.shard_map(
        shards,
        mesh=mesh,
        in_specs=placed,
        out_specs=(P("ctx", "cand"), P("ctx", "cand")),
        check_vma=False,
    )
```

time: 446 us -> 152 us (0.34)
  the two profiles are of different devices: /device:TPU:1 before, /device:TPU:3 now
where the time goes in v2:
time: 152 us
  Pallas kernels  144 us (95%)
  local copies, waits for them, and re-layouts  6.78 us (4%)
    pallas_call x1, Pallas kernels, shards(): pl.pallas_call(kernel, out_shape=(jax.ShapeDtypeStruct((1024, 256), BF16)...  144 us
    unnamed x3, local copies, waits for them, and re-layouts  6.78 us

profile of v2, /device:TPU:3, one launch (start us, length us, event | category | flops | bytes accessed | tf_op | source)
XLA Modules:
  0.0 151.8 jit_solution(6672140838180429417)
XLA Ops:
  0.6 3.4 %copy.12 = bf16[128,8,4,256]{3,1,2,0:T(8,128)(2,1)} copy(bf16[128,8,4,256]{3,2,1,0:T(4,128)(2,1)} %bitcast.9) | data formatting | bytes 4194304
  4.1 144.4 %hstu.1 = (bf16[1024,256]{1,0:T(8,128)(2,1)}, bf16[128,256]{1,0:T(8,128)(2,1)}) custom-call(bf16[1024,1024]{1,0:T(8,128)(2,1)} %x_ref.1, bf16[128,1024]{1,0:T(8,128)(2,1)} %cx_ref.1, s32[8,128]{1,0:T(8,128)} %bitcast.10, s32[8,128]{1,0:T(8,128)} %bitcast.11, s32[1,128]{1,0:T(1,128)} %bitcast.14, s32[1,128]{1,0:T(1,128)} %bitcast.15, f32[1,1024]{1,0:T(1,128)} %bitcast.12, ...), custom_call_target="tpu_custom_call" | custom-call | tf_op jit(solution)/shard_map/hstu/pallas_call | solution.py:344
  148.5 1.9 %copy.15 = bf16[1024,256]{1,0:T(8,128)(2,1)} copy(bf16[1024,256]{1,0:T(8,128)(2,1)} %get-tuple-element.4) | data formatting | bytes 1048576
  150.3 1.5 copy.16

commit v3 on v2

v3 whole, which is shorter than its diff:
```python
import functools
import math

import jax
import jax.numpy as jnp
from jax import lax
from jax.experimental import pallas as pl
from jax.experimental.pallas import tpu as pltpu
from jax.sharding import PartitionSpec as P

HEAD = 128
EPS = 1e-05
HALF_SCALE = 0.5 / math.sqrt(HEAD)
FAR = 2.0**60
CHUNK = 256
CARDS = 128
META = 16
BF16 = jnp.bfloat16
F32 = jnp.float32
MESH = pl.DeviceIdType.MESH
NT = (((1,), (1,)), ((), ()))

N_SEM = 96


def silu_of_half(half):
    return half * jnp.tanh(half) + half


def kernel(
    x_ref, cx_ref, valid_ref, hsurf_ref, csurf_ref, ccut_ref, gin_ref, w_ref, gout_ref, wo_ref,
    oh_ref, oc_ref,
    nq, hx, hv, kv, hkv, qh, uh, cp, kf, qall, qf, lcb, own, pz, rz, px, rx, py, ry, attn, cattn, st, gf, wc,
    ssem, rsem,
):
    c = lax.axis_index("ctx")
    h = lax.axis_index("cand")
    yh, z, xx = c // 16, (c // 4) % 4, c % 4

    def at_x(d):
        return (yh * 16 + z * 4 + (xx + d + 4) % 4, h)

    def at_z(d):
        return (yh * 16 + ((z + d + 4) % 4) * 4 + xx, h)

    def at_y():
        return ((c + 16) % 32, h)

    def at_c(d):
        return ((c + d + 32) % 32, h)

    def at_h(d):
        return (c, (h + d) % 4)

    core_peer = (c, h + 1 - 2 * (h % 2))
    y_peer = (c, (h + 2) % 4)

    barrier = pltpu.get_barrier_semaphore()
    greeted = [at_h(1), at_h(2), at_h(3), at_y(), at_x(1), at_x(2), at_x(3), at_z(1), at_z(2), at_z(3)]
    greeted += [at_c(1), at_c(2), at_c(-1), at_c(-2)]
    for device in greeted:
        pl.semaphore_signal(barrier, inc=1, device_id=device, device_id_type=MESH)

    sent = []

    def send(src, dst, device):
        slot = len(sent)
        copy = pltpu.make_async_remote_copy(
            src_ref=src, dst_ref=dst, send_sem=ssem.at[slot], recv_sem=rsem.at[slot],
            device_id=device, device_id_type=MESH,
        )
        copy.start()
        sent.append(copy)
        return copy

    def normalize(rows):
        values = rows.astype(F32)
        center = values - jnp.mean(values, axis=-1, keepdims=True)
        spread = jnp.mean(center * center, axis=-1, keepdims=True)
        return (center * lax.rsqrt(spread + EPS) * gin_ref[...]).astype(BF16)

    def project(normed, weights):
        half = jnp.dot(normed, weights, preferred_element_type=F32) * 0.5
        return silu_of_half(half).astype(BF16)

    quarter = pl.ds(pl.multiple_of(h * 256, 256), 256)
    nq[...] = normalize(x_ref[quarter, :])

    cp[...] = project(normalize(cx_ref[...]), w_ref[...])
    for head in range(2):
        qall[head, 0, 0, 0, 0:CARDS, :] = cp[:, 512 + head * 128 : 640 + head * 128]
    cut = ccut_ref[...]
    row = lax.broadcasted_iota(jnp.int32, (META, 128), 0)
    told = jnp.where(row == 0, lax.shift_right_logical(cut, 8), cut & 255)
    told = jnp.where(row == 2, csurf_ref[...], told).astype(F32).astype(BF16)
    for head in range(2):
        qall[head, 0, 0, 0, CARDS:, :] = told

    pl.semaphore_wait(barrier, len(greeted))
    near, far = (at_x, at_z), (at_z, at_x)
    q_y = send(qall.at[:, 0, 0, 0], qall.at[:, 0, 0, 1], at_y())
    okay_in = [send(valid_ref, hv.at[b], at_c(b + 1)) for b in (0, 1)]

    def part(quarter_of, k):
        return pl.ds(pl.multiple_of(quarter_of * 256 + k * 128, 128), 128)

    def halo_first(k):
        return send(nq.at[pl.ds(k * 128, 128), :], hx.at[0, part(h, k), :], at_c(1))

    halo_in = {(0, 0): halo_first(0)}

    lane = lax.broadcasted_iota(jnp.int32, (CARDS, 128), 1).astype(F32)
    surf_t = jnp.transpose(hsurf_ref[...].astype(F32))
    for i in range(8):
        kf[i * 128 : i * 128 + 128, :] = jnp.where(surf_t[:, i : i + 1] == lane, 1.0, 0.0).astype(BF16)

    def only_valid(values, flags, i):
        columns = jnp.transpose(flags.astype(F32))
        okay = jnp.concatenate([columns[:, 2 * i : 2 * i + 1], columns[:, 2 * i + 1 : 2 * i + 2]], 0)
        return (values.astype(F32) * okay).astype(BF16)

    def hist_chunk(i):
        at = slice(i * CHUNK, i * CHUNK + CHUNK)
        proj = project(normalize(x_ref[at, :]), w_ref[...])
        uh[at, :] = proj[:, 0:256]
        qh[at, :] = proj[:, 512:768]
        kv[at, 0:256] = proj[:, 768:1024]
        kv[at, 256:512] = only_valid(proj[:, 256:512], valid_ref[...], i)

    hist_chunk(0)
    q_y.wait_recv()
    q_near = []
    for head in range(2):
        for d in (1, 3, 2):
            q_near.append(send(qall.at[head, 0, 0], qall.at[head, 0, d], near[head](d)))
    q_far = {(head, d): [] for head in range(2) for d in (1, 2, 3)}
    for head in range(2):
        for d in (1, 3):
            q_far[head, d].append(send(qall.at[head, 0, 0], qall.at[head, d, 0], far[head](d)))
    halo_in[0, 1] = halo_first(1)
    mine = pl.ds(pl.multiple_of(h * 256, 256), 256)
    hist_chunk(1)
    for copy in q_near:
        copy.wait_recv()
    rest = pl.ds(1, 3)
    for head in range(2):
        for d in (1, 3):
            q_far[head, d].append(
                send(qall.at[head, 0, rest], qall.at[head, d, rest], far[head](d))
            )

    halo_y, halo_core = {}, []

    def halo_pass(b, k):
        halo_in[b, k].wait_recv()
        block = hx.at[b, part(h, k), :]
        if b == 0:
            halo_in[1, k] = send(block, hx.at[1, part(h, k), :], at_c(1))
        halo_y[b, k] = send(block, block, y_peer)
        halo_core.append(send(block, block, core_peer))

    def halo_pass_on(b, k):
        halo_y[b, k].wait_recv()
        block = hx.at[b, part((h + 2) % 4, k), :]
        halo_core.append(send(block, block, core_peer))

    hist_chunk(2)
    halo_pass(0, 0)
    hist_chunk(3)
    for head in range(2):
        for d in (1, 3):
            for copy in q_far[head, d]:
                copy.wait_recv()
            pair = pl.ds(0, 2) if d == 1 else pl.ds(2, 2)
            q_far[head, 2].append(
                send(qall.at[head, d, pair], qall.at[head, 2, pair], far[head](1 if d == 1 else -1))
            )
    halo_pass(0, 1)
    into = []
    for d in (1, 2, 3):
        theirs = pl.ds(pl.multiple_of(((h + d) % 4) * 256, 256), 256)
        into.append(send(wo_ref.at[:, theirs], wc.at[mine, :], at_h(d)))
    wc[mine, :] = wo_ref[:, mine]

    def attend(queries, keys, values, mask):
        half = lax.dot_general(queries, keys, NT, preferred_element_type=F32) * HALF_SCALE
        weights = silu_of_half(half)
        if mask is not None:
            weights = jnp.where(mask(weights.shape), weights, 0.0)
        return jnp.dot(weights.astype(BF16), values, preferred_element_type=F32)

    def hist_tile(keys_ref, j, lo, hi, mask):
        ks = slice(j * CHUNK, j * CHUNK + CHUNK)
        out = []
        for head in range(2):
            a, b = head * 128, head * 128 + 128
            out.append(attend(qh[lo:hi, a:b], keys_ref[ks, a:b], keys_ref[ks, 256 + a : 256 + b], mask))
        return jnp.concatenate(out, 1)

    def not_later(shape):
        return lax.broadcasted_iota(jnp.int32, shape, 1) <= lax.broadcasted_iota(jnp.int32, shape, 0)

    start = (c * 1024).astype(F32)

    def cand_plane(head, d):
        a, b = head * 128, head * 128 + 128
        row = lax.broadcasted_iota(jnp.int32, (8, 128), 0)
        for n in range(4):
            for dy in range(2):
                told = qall[head, d, n, dy, CARDS:, :].astype(F32)
                local = told[0:1, :] * 256.0 + told[1:2, :] - start
                both = jnp.transpose(jnp.where(row == 0, local, told[2:3, :]))
                r = (n * 2 + dy) * 128
                lcb[r : r + 128, :] = jnp.broadcast_to(both[:, 0:1], (128, 128))
                qf[r : r + 128, :] = jnp.where(both[:, 1:2] == lane, 0.0, -FAR).astype(BF16)
        queries = jnp.concatenate(
            [qall[head, d, n, dy, 0:CARDS, :] for n in range(4) for dy in range(2)], 0
        )
        queries = jnp.concatenate([queries, qf[...]], 1)
        total = None
        for j in range(4):
            ks = slice(j * CHUNK, j * CHUNK + CHUNK)
            keys = jnp.concatenate([kv[ks, a:b], kf[ks, :]], 1)

            def mask(shape):
                place = (lax.broadcasted_iota(jnp.int32, shape, 1) + j * CHUNK).astype(F32)
                return place < jnp.concatenate([lcb[...], lcb[...]], 1)

            piece = attend(queries, keys, kv[ks, 256 + a : 256 + b], mask)
            total = piece if total is None else total + piece
        return total

    p_far = []

    def serve(head, d):
        pz[head, d - 1] = cand_plane(head, d).astype(BF16)
        p_far.append(send(pz.at[head, d - 1], rz.at[head, d - 1], far[head](-d)))

    def halo_project(b, i):
        at = slice(i * CHUNK, i * CHUNK + CHUNK)
        weights = jnp.concatenate([w_ref[:, 768:1024], w_ref[:, 256:512]], 1)
        proj = project(hx[b, at, :], weights)
        hkv[b, at, 0:256] = proj[:, 0:256]
        hkv[b, at, 256:512] = only_valid(proj[:, 256:512], hv[b], i)

    serve(0, 1)
    serve(1, 1)
    halo_pass_on(0, 0)
    serve(0, 3)
    serve(1, 3)
    halo_pass(1, 0)
    halo_pass_on(0, 1)
    for head in range(2):
        for copy in q_far[head, 2]:
            copy.wait_recv()
        serve(head, 2)
    halo_pass(1, 1)
    own[0] = cand_plane(0, 0)
    own[1] = cand_plane(1, 0)
    halo_pass_on(1, 0)
    attn[...] = hist_tile(kv, 0, 0, 1024, not_later)
    for j in (1, 2, 3):
        attn[j * CHUNK :, :] += hist_tile(kv, j, j * CHUNK, 1024, not_later)
    halo_pass_on(1, 1)

    for copy in p_far:
        copy.wait_recv()
    p_near = []
    for head in range(2):
        total = own[head]
        for d in (1, 2, 3):
            total += rz[head, d - 1].astype(F32)
        px[head] = total.astype(BF16)
        own[head, 0:256, :] = total[0:256]
        for d in (1, 3, 2):
            p_near.append(
                send(px.at[head, pl.ds(d * 256, 256)], rx.at[head, d - 1], near[head](-d))
            )

    full = 1024.0

    def chunk_rows(i):
        return (slice(i * CHUNK, i * CHUNK + CHUNK), CHUNK) if i < 4 else (slice(1024, 1152), CARDS)

    def stats_out(i, values):
        size = values.shape[0]
        sums = jnp.sum(values, axis=-1, keepdims=True)
        squares = jnp.sum(values * values, axis=-1, keepdims=True)
        spread = lax.broadcasted_iota(jnp.int32, (size, 128), 1)
        st[0, i, :, 0:size] = jnp.transpose(jnp.where(spread == 0, sums, squares))[0:8, :]
        return [send(st.at[0, i], st.at[d, i], at_h(d)) for d in (1, 2, 3)]

    def gate_out(i, values, update, got):
        at, size = chunk_rows(i)
        for copy in got:
            copy.wait_recv()
        both = (st[0, i] + st[1, i] + st[2, i] + st[3, i])[:, 0:size] / full
        both = jnp.transpose(both)
        mean, square = both[:, 0:1], both[:, 1:2]
        gated = (values - mean) * lax.rsqrt(square - mean * mean + EPS) * gout_ref[...] * update.astype(F32)
        gf[at, mine] = gated.astype(BF16)
        block = gf.at[at, mine]
        return [
            send(block, block, core_peer),
            send(block, block, y_peer),
        ]

    across = pl.ds(pl.multiple_of(((h + 2) % 4) * 256, 256), 256)

    def gate_forward(i, moving):
        at, _ = chunk_rows(i)
        moving[1].wait_recv()
        block = gf.at[at, across]
        moving.append(send(block, block, core_peer))

    def finish(i, moving, rows_ref, out_ref):
        at, size = chunk_rows(i)
        moving[0].wait_recv()
        moving[2].wait_recv()
        where = at if i < 4 else slice(0, CARDS)
        mixed = jnp.dot(gf[at, :], wc[...], preferred_element_type=F32)
        out_ref[where, :] = (rows_ref[where, mine].astype(F32) + mixed).astype(BF16)

    got, moving = {}, {}
    for copy in okay_in + halo_core:
        copy.wait_recv()
    for i in range(4):
        halo_project(0, i)
    for copy in p_near:
        copy.wait_recv()
    for head in range(2):
        total = own[head, 0:256, :]
        for d in (1, 2, 3):
            total += rx[head, d - 1].astype(F32)
        own[head, 0:CARDS, :] = total[0:CARDS]
        py[head] = total[CARDS:]
    p_y = send(py, ry, at_y())

    @pl.when(c >= 1)
    def _():
        for j in range(4):
            attn[...] += hist_tile(hkv.at[0], j, 0, 1024, None)

    p_y.wait_recv()
    for head in range(2):
        a, b = head * 128, head * 128 + 128
        query = cp[:, 512 + a : 512 + b].astype(F32)
        key = cp[:, 768 + a : 768 + b].astype(F32)
        half = jnp.sum(query * key, axis=-1, keepdims=True) * HALF_SCALE
        weight = silu_of_half(half).astype(BF16).astype(F32)
        term = weight * cp[:, 256 + a : 256 + b].astype(F32)
        cattn[:, a:b] = own[head, 0:CARDS, :] + ry[head] + term
    got[4] = stats_out(4, cattn[...])
    for i in range(4):
        halo_project(1, i)
    moving[4] = gate_out(4, cattn[...], cp[:, 0:256], got[4])

    for i in (3, 2, 1, 0):

        @pl.when(c >= 2)
        def _():
            def later(shape):
                return (
                    lax.broadcasted_iota(jnp.int32, shape, 1) + i * CHUNK
                    > lax.broadcasted_iota(jnp.int32, shape, 0)
                )

            hi = i * CHUNK + CHUNK
            attn[0:hi, :] += hist_tile(hkv.at[1], i, 0, hi, later)

        got[i] = stats_out(i, attn[chunk_rows(i)[0], :])

    def gate_hist(i):
        where = chunk_rows(i)[0]
        moving[i] = gate_out(i, attn[where, :], uh[where, :], got[i])

    for copy in into:
        copy.wait_recv()
    gate_hist(3)
    gate_hist(2)
    gate_forward(4, moving[4])
    gate_hist(1)
    gate_hist(0)
    gate_forward(3, moving[3])
    finish(4, moving[4], cx_ref, oc_ref)
    gate_forward(2, moving[2])
    finish(3, moving[3], x_ref, oh_ref)
    gate_forward(1, moving[1])
    finish(2, moving[2], x_ref, oh_ref)
    gate_forward(0, moving[0])
    finish(1, moving[1], x_ref, oh_ref)
    finish(0, moving[0], x_ref, oh_ref)
    for copy in sent:
        copy.wait_send()


def shards(
    history,
    candidates,
    history_valid,
    history_surface,
    candidate_surface,
    candidate_cutoff,
    gain_in,
    w_uvqk,
    gain_out,
    w_out,
):
    vmem = pl.BlockSpec(memory_space=pltpu.VMEM)
    return pl.pallas_call(
        kernel,
        out_shape=(
            jax.ShapeDtypeStruct((1024, 256), BF16),
            jax.ShapeDtypeStruct((CARDS, 256), BF16),
        ),
        in_specs=[vmem] * 10,
        out_specs=(vmem, vmem),
        scratch_shapes=[
            pltpu.VMEM((256, 1024), BF16),
            pltpu.VMEM((2, 1024, 1024), BF16),
            pltpu.VMEM((2, 8, 128), jnp.int32),
            pltpu.VMEM((1024, 512), BF16),
            pltpu.VMEM((2, 1024, 512), BF16),
            pltpu.VMEM((1024, 256), BF16),
            pltpu.VMEM((1024, 256), BF16),
            pltpu.VMEM((CARDS, 1024), BF16),
            pltpu.VMEM((1024, 128), BF16),
            pltpu.VMEM((2, 4, 4, 2, CARDS + META, 128), BF16),
            pltpu.VMEM((1024, 128), BF16),
            pltpu.VMEM((1024, 128), F32),
            pltpu.VMEM((2, 1024, 128), F32),
            pltpu.VMEM((2, 3, 1024, 128), BF16),
            pltpu.VMEM((2, 3, 1024, 128), BF16),
            pltpu.VMEM((2, 1024, 128), BF16),
            pltpu.VMEM((2, 3, 256, 128), BF16),
            pltpu.VMEM((2, CARDS, 128), F32),
            pltpu.VMEM((2, CARDS, 128), F32),
            pltpu.VMEM((1024, 256), F32),
            pltpu.VMEM((CARDS, 256), F32),
            pltpu.VMEM((4, 5, 8, 256), F32),
            pltpu.VMEM((1152, 1024), BF16),
            pltpu.VMEM((1024, 256), BF16),
            pltpu.SemaphoreType.DMA((N_SEM,)),
            pltpu.SemaphoreType.DMA((N_SEM,)),
        ],
        compiler_params=pltpu.CompilerParams(
            collective_id=0, has_side_effects=True, vmem_limit_bytes=56 * 2**20
        ),
        name="hstu",
    )(
        history,
        candidates,
        history_valid.reshape(8, 128),
        history_surface.reshape(8, 128),
        candidate_surface.reshape(1, CARDS),
        candidate_cutoff.reshape(1, CARDS),
        gain_in.reshape(1, 1024),
        w_uvqk.reshape(1024, 1024),
        gain_out.reshape(1, 256),
        w_out,
    )


def solution(mesh):
    placed = (
        P("ctx", None),
        P("ctx", None),
        P("ctx"),
        P("ctx"),
        P("ctx"),
        P("ctx"),
        P(),
        P(None, None, "cand"),
        P("cand"),
        P("cand", None),
    )
    return jax.shard_map(
        shards,
        mesh=mesh,
        in_specs=placed,
        out_specs=(P("ctx", "cand"), P("ctx", "cand")),
        check_vma=False,
    )
```

time: 152 us -> 110 us (0.72)
  the two profiles are of different devices: /device:TPU:3 before, /device:TPU:1 now
where the time goes in v3:
time: 110 us
  Pallas kernels  102 us (93%)
  local copies, waits for them, and re-layouts  6.78 us (6%)
    pallas_call x1, Pallas kernels, shards(): pl.pallas_call(kernel, out_shape=(jax.ShapeDtypeStruct((1024, 256), BF16)...  102 us
    unnamed x3, local copies, waits for them, and re-layouts  6.78 us

profile of v3, /device:TPU:1, one launch (start us, length us, event | category | flops | bytes accessed | tf_op | source)
XLA Modules:
  0.0 109.5 jit_solution(12878230004045071675)
XLA Ops:
  0.6 3.4 %copy.12 = bf16[128,8,4,256]{3,1,2,0:T(8,128)(2,1)} copy(bf16[128,8,4,256]{3,2,1,0:T(4,128)(2,1)} %bitcast.9) | data formatting | bytes 4194304
  4.1 102.1 %hstu.1 = (bf16[1024,256]{1,0:T(8,128)(2,1)}, bf16[128,256]{1,0:T(8,128)(2,1)}) custom-call(bf16[1024,1024]{1,0:T(8,128)(2,1)} %x_ref.1, bf16[128,1024]{1,0:T(8,128)(2,1)} %cx_ref.1, s32[8,128]{1,0:T(8,128)} %bitcast.10, s32[8,128]{1,0:T(8,128)} %bitcast.11, s32[1,128]{1,0:T(1,128)} %bitcast.14, s32[1,128]{1,0:T(1,128)} %bitcast.15, f32[1,1024]{1,0:T(1,128)} %bitcast.12, ...), custom_call_target="tpu_custom_call" | custom-call | tf_op jit(solution)/shard_map/hstu/pallas_call | solution.py:410
  106.2 1.9 %copy.15 = bf16[1024,256]{1,0:T(8,128)(2,1)} copy(bf16[1024,256]{1,0:T(8,128)(2,1)} %get-tuple-element.4) | data formatting | bytes 1048576
  108.0 1.5 %copy.16 = bf16[128,256]{1,0:T(8,128)(2,1)} copy(bf16[128,256]{1,0:T(8,128)(2,1)} %get-tuple-element.5) | data formatting | bytes 131072

commit v4 on v3

--- a/solution.py
+++ b/solution.py
@@ -63,15 +63,30 @@
 
     sent = []
 
-    def send(src, dst, device):
-        slot = len(sent)
-        copy = pltpu.make_async_remote_copy(
-            src_ref=src, dst_ref=dst, send_sem=ssem.at[slot], recv_sem=rsem.at[slot],
-            device_id=device, device_id_type=MESH,
-        )
-        copy.start()
-        sent.append(copy)
-        return copy
+    class Transfer:
+        def __init__(self, src, dst, device, sends=None, receives=None):
+            slot = len(sent)
+            self.copy = pltpu.make_async_remote_copy(
+                src_ref=src, dst_ref=dst, send_sem=ssem.at[slot], recv_sem=rsem.at[slot],
+                device_id=device, device_id_type=MESH,
+            )
+            self.sends, self.receives = sends, receives
+            sent.append(self)
+            self.only(sends, self.copy.start)
+
+        def only(self, condition, act):
+            if condition is None:
+                act()
+            else:
+                pl.when(condition)(lambda: act())
+
+        def wait_recv(self):
+            self.only(self.receives, self.copy.wait_recv)
+
+        def wait_send(self):
+            self.only(self.sends, self.copy.wait_send)
+
+    send = Transfer
 
     def normalize(rows):
         values = rows.astype(F32)
@@ -83,8 +98,9 @@
         half = jnp.dot(normed, weights, preferred_element_type=F32) * 0.5
         return silu_of_half(half).astype(BF16)
 
-    quarter = pl.ds(pl.multiple_of(h * 256, 256), 256)
-    nq[...] = normalize(x_ref[quarter, :])
+    for i in range(4):
+        quarter = pl.ds(pl.multiple_of(i * CHUNK + h * 64, 64), 64)
+        nq[i * 64 : i * 64 + 64, :] = normalize(x_ref[quarter, :])
 
     cp[...] = project(normalize(cx_ref[...]), w_ref[...])
     for head in range(2):
@@ -101,13 +117,15 @@
     q_y = send(qall.at[:, 0, 0, 0], qall.at[:, 0, 0, 1], at_y())
     okay_in = [send(valid_ref, hv.at[b], at_c(b + 1)) for b in (0, 1)]
 
-    def part(quarter_of, k):
-        return pl.ds(pl.multiple_of(quarter_of * 256 + k * 128, 128), 128)
-
-    def halo_first(k):
-        return send(nq.at[pl.ds(k * 128, 128), :], hx.at[0, part(h, k), :], at_c(1))
-
-    halo_in = {(0, 0): halo_first(0)}
+    def part(quarter_of, i):
+        return pl.ds(pl.multiple_of(i * CHUNK + quarter_of * 64, 64), 64)
+
+    def halo_first(i):
+        rows = nq.at[pl.ds(i * 64, 64), :]
+        return send(rows, hx.at[0, part(h, i), :], at_c(1), c <= 30, c >= 1)
+
+    halo_in = {(0, i): halo_first(i) for i in (3, 2, 1, 0)}
+    mine = pl.ds(pl.multiple_of(h * 256, 256), 256)
 
     lane = lax.broadcasted_iota(jnp.int32, (CARDS, 128), 1).astype(F32)
     surf_t = jnp.transpose(hsurf_ref[...].astype(F32))
@@ -136,51 +154,41 @@
     q_far = {(head, d): [] for head in range(2) for d in (1, 2, 3)}
     for head in range(2):
         for d in (1, 3):
-            q_far[head, d].append(send(qall.at[head, 0, 0], qall.at[head, d, 0], far[head](d)))
-    halo_in[0, 1] = halo_first(1)
-    mine = pl.ds(pl.multiple_of(h * 256, 256), 256)
-    hist_chunk(1)
+            pass
+    for i in (1, 2, 3):
+        hist_chunk(i)
+    halo_y, halo_core = {}, {}
+
+    def halo_pass(b, i):
+        halo_in[b, i].wait_recv()
+        block = hx.at[b, part(h, i), :]
+        known = c >= b + 1
+        if b == 0:
+            halo_in[1, i] = send(
+                block, hx.at[1, part(h, i), :], at_c(1), (c >= 1) & (c <= 30), c >= 2
+            )
+        halo_y[b, i] = send(block, block, y_peer, known, known)
+        halo_core[b, i] = [send(block, block, core_peer, known, known)]
+
+    def halo_pass_on(b, i):
+        halo_y[b, i].wait_recv()
+        block = hx.at[b, part((h + 2) % 4, i), :]
+        known = c >= b + 1
+        halo_core[b, i].append(send(block, block, core_peer, known, known))
+
+    def halo_whole(b, i):
+        for copy in halo_core[b, i]:
+            copy.wait_recv()
+
+    for i in (3, 2, 1, 0):
+        halo_pass(0, i)
     for copy in q_near:
         copy.wait_recv()
-    rest = pl.ds(1, 3)
     for head in range(2):
         for d in (1, 3):
             q_far[head, d].append(
-                send(qall.at[head, 0, rest], qall.at[head, d, rest], far[head](d))
+                send(qall.at[head, 0], qall.at[head, d], far[head](d))
             )
-
-    halo_y, halo_core = {}, []
-
-    def halo_pass(b, k):
-        halo_in[b, k].wait_recv()
-        block = hx.at[b, part(h, k), :]
-        if b == 0:
-            halo_in[1, k] = send(block, hx.at[1, part(h, k), :], at_c(1))
-        halo_y[b, k] = send(block, block, y_peer)
-        halo_core.append(send(block, block, core_peer))
-
-    def halo_pass_on(b, k):
-        halo_y[b, k].wait_recv()
-        block = hx.at[b, part((h + 2) % 4, k), :]
-        halo_core.append(send(block, block, core_peer))
-
-    hist_chunk(2)
-    halo_pass(0, 0)
-    hist_chunk(3)
-    for head in range(2):
-        for d in (1, 3):
-            for copy in q_far[head, d]:
-                copy.wait_recv()
-            pair = pl.ds(0, 2) if d == 1 else pl.ds(2, 2)
-            q_far[head, 2].append(
-                send(qall.at[head, d, pair], qall.at[head, 2, pair], far[head](1 if d == 1 else -1))
-            )
-    halo_pass(0, 1)
-    into = []
-    for d in (1, 2, 3):
-        theirs = pl.ds(pl.multiple_of(((h + d) % 4) * 256, 256), 256)
-        into.append(send(wo_ref.at[:, theirs], wc.at[mine, :], at_h(d)))
-    wc[mine, :] = wo_ref[:, mine]
 
     def attend(queries, keys, values, mask):
         half = lax.dot_general(queries, keys, NT, preferred_element_type=F32) * HALF_SCALE
@@ -243,25 +251,51 @@
         hkv[b, at, 0:256] = proj[:, 0:256]
         hkv[b, at, 256:512] = only_valid(proj[:, 256:512], hv[b], i)
 
+    attn[...] = hist_tile(kv, 0, 0, 1024, not_later)
+    for j in (1, 2, 3):
+        attn[j * CHUNK :, :] += hist_tile(kv, j, j * CHUNK, 1024, not_later)
+    own[0] = cand_plane(0, 0)
+    for i in (3, 2):
+        halo_pass_on(0, i)
+        halo_pass(1, i)
+    for i in (1, 0):
+        halo_pass_on(0, i)
+        halo_pass(1, i)
+    for head in range(2):
+        for d in (1, 3):
+            for copy in q_far[head, d]:
+                copy.wait_recv()
+    for d, blocks in ((1, pl.ds(0, 2)), (3, pl.ds(2, 2))):
+        q_far[0, 2].append(send(qall.at[0, d, blocks], qall.at[0, 2, blocks], at_z(2 - d)))
+        q_far[1, 2].append(send(qall.at[1, d, blocks], qall.at[1, 2, blocks], at_x(2 - d)))
     serve(0, 1)
     serve(1, 1)
-    halo_pass_on(0, 0)
     serve(0, 3)
     serve(1, 3)
-    halo_pass(1, 0)
-    halo_pass_on(0, 1)
     for head in range(2):
         for copy in q_far[head, 2]:
             copy.wait_recv()
         serve(head, 2)
-    halo_pass(1, 1)
-    own[0] = cand_plane(0, 0)
+    for i in (3, 2, 1, 0):
+        halo_pass_on(1, i)
     own[1] = cand_plane(1, 0)
-    halo_pass_on(1, 0)
-    attn[...] = hist_tile(kv, 0, 0, 1024, not_later)
-    for j in (1, 2, 3):
-        attn[j * CHUNK :, :] += hist_tile(kv, j, j * CHUNK, 1024, not_later)
-    halo_pass_on(1, 1)
+    into = []
+    for d in (1, 2, 3):
+        theirs = pl.ds(pl.multiple_of(((h + d) % 4) * 256, 256), 256)
+        into.append(send(wo_ref.at[:, theirs], wc.at[mine, :], at_h(d)))
+    wc[mine, :] = wo_ref[:, mine]
+
+    for copy in okay_in:
+        copy.wait_recv()
+    for i in range(4):
+        halo_whole(0, i)
+    for i in range(4):
+        halo_project(0, i)
+
+    @pl.when(c >= 1)
+    def _():
+        for j in range(4):
+            attn[...] += hist_tile(hkv.at[0], j, 0, 1024, None)
 
     for copy in p_far:
         copy.wait_recv()
@@ -322,40 +356,9 @@
         out_ref[where, :] = (rows_ref[where, mine].astype(F32) + mixed).astype(BF16)
 
     got, moving = {}, {}
-    for copy in okay_in + halo_core:
-        copy.wait_recv()
-    for i in range(4):
-        halo_project(0, i)
-    for copy in p_near:
-        copy.wait_recv()
-    for head in range(2):
-        total = own[head, 0:256, :]
-        for d in (1, 2, 3):
-            total += rx[head, d - 1].astype(F32)
-        own[head, 0:CARDS, :] = total[0:CARDS]
-        py[head] = total[CARDS:]
-    p_y = send(py, ry, at_y())
-
-    @pl.when(c >= 1)
-    def _():
-        for j in range(4):
-            attn[...] += hist_tile(hkv.at[0], j, 0, 1024, None)
-
-    p_y.wait_recv()
-    for head in range(2):
-        a, b = head * 128, head * 128 + 128
-        query = cp[:, 512 + a : 512 + b].astype(F32)
-        key = cp[:, 768 + a : 768 + b].astype(F32)
-        half = jnp.sum(query * key, axis=-1, keepdims=True) * HALF_SCALE
-        weight = silu_of_half(half).astype(BF16).astype(F32)
-        term = weight * cp[:, 256 + a : 256 + b].astype(F32)
-        cattn[:, a:b] = own[head, 0:CARDS, :] + ry[head] + term
-    got[4] = stats_out(4, cattn[...])
-    for i in range(4):
+    for i in (3, 2, 1, 0):
+        halo_whole(1, i)
         halo_project(1, i)
-    moving[4] = gate_out(4, cattn[...], cp[:, 0:256], got[4])
-
-    for i in (3, 2, 1, 0):
 
         @pl.when(c >= 2)
         def _():
@@ -374,22 +377,45 @@
         where = chunk_rows(i)[0]
         moving[i] = gate_out(i, attn[where, :], uh[where, :], got[i])
 
-    for copy in into:
+    for copy in p_near:
         copy.wait_recv()
+    for head in range(2):
+        total = own[head, 0:256, :]
+        for d in (1, 2, 3):
+            total += rx[head, d - 1].astype(F32)
+        own[head, 0:CARDS, :] = total[0:CARDS]
+        py[head] = total[CARDS:]
+    p_y = send(py, ry, at_y())
     gate_hist(3)
     gate_hist(2)
-    gate_forward(4, moving[4])
+    selfs = []
+    for head in range(2):
+        a, b = head * 128, head * 128 + 128
+        query = cp[:, 512 + a : 512 + b].astype(F32)
+        key = cp[:, 768 + a : 768 + b].astype(F32)
+        half = jnp.sum(query * key, axis=-1, keepdims=True) * HALF_SCALE
+        weight = silu_of_half(half).astype(BF16).astype(F32)
+        selfs.append(weight * cp[:, 256 + a : 256 + b].astype(F32))
+    p_y.wait_recv()
+    for head in range(2):
+        a, b = head * 128, head * 128 + 128
+        cattn[:, a:b] = own[head, 0:CARDS, :] + ry[head] + selfs[head]
+    got[4] = stats_out(4, cattn[...])
     gate_hist(1)
     gate_hist(0)
     gate_forward(3, moving[3])
-    finish(4, moving[4], cx_ref, oc_ref)
+    moving[4] = gate_out(4, cattn[...], cp[:, 0:256], got[4])
+    for copy in into:
+        copy.wait_recv()
     gate_forward(2, moving[2])
     finish(3, moving[3], x_ref, oh_ref)
     gate_forward(1, moving[1])
     finish(2, moving[2], x_ref, oh_ref)
     gate_forward(0, moving[0])
     finish(1, moving[1], x_ref, oh_ref)
+    gate_forward(4, moving[4])
     finish(0, moving[0], x_ref, oh_ref)
+    finish(4, moving[4], cx_ref, oc_ref)
     for copy in sent:
         copy.wait_send()
 

time: 110 us -> 100 us (0.909)
  Pallas kernels: 102 us -> 92.5 us
    pallas_call x1, Pallas kernels: 102 us -> 92.5 us  [shards(): pl.pallas_call(kernel, out_shape=(jax.ShapeDtypeStruct((1024, 256), BF16)...]
where the time goes in v4:
time: 100 us; the launch traced here: 99.9 us
  Pallas kernels  92.5 us (92%)
  local copies, waits for them, and re-layouts  6.78 us (7%)
    pallas_call x1, Pallas kernels, shards(): pl.pallas_call(kernel, out_shape=(jax.ShapeDtypeStruct((1024, 256), BF16)...  92.5 us
    unnamed x3, local copies, waits for them, and re-layouts  6.78 us

profile of v4, /device:TPU:1, one launch (start us, length us, event | category | flops | bytes accessed | tf_op | source)
XLA Modules:
  0.0 99.9 jit_solution(10587587293258194712)
XLA Ops:
  0.6 3.4 %copy.12 = bf16[128,8,4,256]{3,1,2,0:T(8,128)(2,1)} copy(bf16[128,8,4,256]{3,2,1,0:T(4,128)(2,1)} %bitcast.9) | data formatting | bytes 4194304
  4.1 92.5 %hstu.1 = (bf16[1024,256]{1,0:T(8,128)(2,1)}, bf16[128,256]{1,0:T(8,128)(2,1)}) custom-call(bf16[1024,1024]{1,0:T(8,128)(2,1)} %x_ref.1, bf16[128,1024]{1,0:T(8,128)(2,1)} %cx_ref.1, s32[8,128]{1,0:T(8,128)} %bitcast.10, s32[8,128]{1,0:T(8,128)} %bitcast.11, s32[1,128]{1,0:T(1,128)} %bitcast.14, s32[1,128]{1,0:T(1,128)} %bitcast.15, f32[1,1024]{1,0:T(1,128)} %bitcast.12, ...), custom_call_target="tpu_custom_call" | custom-call | tf_op jit(solution)/shard_map/hstu/pallas_call | solution.py:436
  96.5 1.9 %copy.15 = bf16[1024,256]{1,0:T(8,128)(2,1)} copy(bf16[1024,256]{1,0:T(8,128)(2,1)} %get-tuple-element.4) | data formatting | bytes 1048576
  98.4 1.5 %copy.16 = bf16[128,256]{1,0:T(8,128)(2,1)} copy(bf16[128,256]{1,0:T(8,128)(2,1)} %get-tuple-element.5) | data formatting | bytes 131072

commit v5 on v4

--- a/solution.py
+++ b/solution.py
@@ -30,7 +30,7 @@
 def kernel(
     x_ref, cx_ref, valid_ref, hsurf_ref, csurf_ref, ccut_ref, gin_ref, w_ref, gout_ref, wo_ref,
     oh_ref, oc_ref,
-    nq, hx, hv, kv, hkv, qh, uh, cp, kf, qall, qf, lcb, own, pz, rz, px, rx, py, ry, attn, cattn, st, gf, wc,
+    ws, nq, hx, hv, kv, hkv, qh, uh, cp, kf, qall, qf, lcb, own, pz, rz, px, rx, py, ry, attn, cattn, st, gf, wc,
     ssem, rsem,
 ):
     c = lax.axis_index("ctx")
@@ -98,11 +98,13 @@
         half = jnp.dot(normed, weights, preferred_element_type=F32) * 0.5
         return silu_of_half(half).astype(BF16)
 
+    ws[...] = w_ref[...].reshape(1024, 1024)
+
     for i in range(4):
         quarter = pl.ds(pl.multiple_of(i * CHUNK + h * 64, 64), 64)
         nq[i * 64 : i * 64 + 64, :] = normalize(x_ref[quarter, :])
 
-    cp[...] = project(normalize(cx_ref[...]), w_ref[...])
+    cp[...] = project(normalize(cx_ref[...]), ws[...])
     for head in range(2):
         qall[head, 0, 0, 0, 0:CARDS, :] = cp[:, 512 + head * 128 : 640 + head * 128]
     cut = ccut_ref[...]
@@ -139,7 +141,7 @@
 
     def hist_chunk(i):
         at = slice(i * CHUNK, i * CHUNK + CHUNK)
-        proj = project(normalize(x_ref[at, :]), w_ref[...])
+        proj = project(normalize(x_ref[at, :]), ws[...])
         uh[at, :] = proj[:, 0:256]
         qh[at, :] = proj[:, 512:768]
         kv[at, 0:256] = proj[:, 768:1024]
@@ -246,7 +248,7 @@
 
     def halo_project(b, i):
         at = slice(i * CHUNK, i * CHUNK + CHUNK)
-        weights = jnp.concatenate([w_ref[:, 768:1024], w_ref[:, 256:512]], 1)
+        weights = jnp.concatenate([ws[:, 768:1024], ws[:, 256:512]], 1)
         proj = project(hx[b, at, :], weights)
         hkv[b, at, 0:256] = proj[:, 0:256]
         hkv[b, at, 256:512] = only_valid(proj[:, 256:512], hv[b], i)
@@ -442,6 +444,7 @@
         in_specs=[vmem] * 10,
         out_specs=(vmem, vmem),
         scratch_shapes=[
+            pltpu.VMEM((1024, 1024), BF16),
             pltpu.VMEM((256, 1024), BF16),
             pltpu.VMEM((2, 1024, 1024), BF16),
             pltpu.VMEM((2, 8, 128), jnp.int32),
@@ -481,7 +484,7 @@
         candidate_surface.reshape(1, CARDS),
         candidate_cutoff.reshape(1, CARDS),
         gain_in.reshape(1, 1024),
-        w_uvqk.reshape(1024, 1024),
+        w_uvqk,
         gain_out.reshape(1, 256),
         w_out,
     )

time: 100 us -> 96.7 us (0.967)
  local copies, waits for them, and re-layouts: 6.78 us -> 3.34 us
    unnamed x3 -> x2, local copies, waits for them, and re-layouts: 6.78 us -> 3.34 us
where the time goes in v5:
time: 96.7 us; the launch traced here: 96.5 us
  Pallas kernels  92.5 us (96%)
  local copies, waits for them, and re-layouts  3.34 us (3%)
    pallas_call x1, Pallas kernels, shards(): pl.pallas_call(kernel, out_shape=(jax.ShapeDtypeStruct((1024, 256), BF16)...  92.5 us
    unnamed x2, local copies, waits for them, and re-layouts  3.34 us

profile of v5, /device:TPU:1, one launch (start us, length us, event | category | flops | bytes accessed | tf_op | source)
XLA Modules:
  0.0 96.5 jit_solution(13137554129507773400)
XLA Ops:
  0.6 92.5 %hstu.1 = (bf16[1024,256]{1,0:T(8,128)(2,1)}, bf16[128,256]{1,0:T(8,128)(2,1)}) custom-call(bf16[1024,1024]{1,0:T(8,128)(2,1)} %x_ref.1, bf16[128,1024]{1,0:T(8,128)(2,1)} %cx_ref.1, s32[8,128]{1,0:T(8,128)} %bitcast.6, s32[8,128]{1,0:T(8,128)} %bitcast.7, s32[1,128]{1,0:T(1,128)} %bitcast.10, s32[1,128]{1,0:T(1,128)} %bitcast.11, f32[1,1024]{1,0:T(1,128)} %bitcast.8, ...), custom_call_target="tpu_custom_call" | custom-call | tf_op jit(solution)/shard_map/hstu/pallas_call | solution.py:438
  93.2 1.9 %copy.14 = bf16[1024,256]{1,0:T(8,128)(2,1)} copy(bf16[1024,256]{1,0:T(8,128)(2,1)} %get-tuple-element.4) | data formatting | bytes 1048576
  95.0 1.5 %copy.15 = bf16[128,256]{1,0:T(8,128)(2,1)} copy(bf16[128,256]{1,0:T(8,128)(2,1)} %get-tuple-element.5) | data formatting | bytes 131072

commit v6 on v5

--- a/solution.py
+++ b/solution.py
@@ -28,10 +28,10 @@
 
 
 def kernel(
-    x_ref, cx_ref, valid_ref, hsurf_ref, csurf_ref, ccut_ref, gin_ref, w_ref, gout_ref, wo_ref,
+    x_hbm, cx_ref, valid_ref, hsurf_ref, csurf_ref, ccut_ref, gin_ref, w_hbm, gout_ref, wo_hbm,
     oh_ref, oc_ref,
-    ws, nq, hx, hv, kv, hkv, qh, uh, cp, kf, qall, qf, lcb, own, pz, rz, px, rx, py, ry, attn, cattn, st, gf, wc,
-    ssem, rsem,
+    x_ref, w_ref, wo_ref, ws, nq, hx, hv, kv, hkv, qh, uh, cp, kf, qall, qf, lcb, own, pz, rz, px, rx, py, ry, attn, cattn, st, gf, wc,
+    ssem, rsem, lsem,
 ):
     c = lax.axis_index("ctx")
     h = lax.axis_index("cand")
@@ -61,6 +61,12 @@
     for device in greeted:
         pl.semaphore_signal(barrier, inc=1, device_id=device, device_id_type=MESH)
 
+    loads = [
+        pltpu.make_async_copy(src, dst, lsem.at[i])
+        for i, (src, dst) in enumerate([(w_hbm, w_ref), (x_hbm, x_ref), (wo_hbm, wo_ref)])
+    ]
+    for load in loads:
+        load.start()
     sent = []
 
     class Transfer:
@@ -98,7 +104,10 @@
         half = jnp.dot(normed, weights, preferred_element_type=F32) * 0.5
         return silu_of_half(half).astype(BF16)
 
+    loads[0].wait()
     ws[...] = w_ref[...].reshape(1024, 1024)
+    loads[1].wait()
+    loads[2].wait()
 
     for i in range(4):
         quarter = pl.ds(pl.multiple_of(i * CHUNK + h * 64, 64), 64)
@@ -435,15 +444,19 @@
     w_out,
 ):
     vmem = pl.BlockSpec(memory_space=pltpu.VMEM)
+    hbm = pl.BlockSpec(memory_space=pl.ANY)
     return pl.pallas_call(
         kernel,
         out_shape=(
             jax.ShapeDtypeStruct((1024, 256), BF16),
             jax.ShapeDtypeStruct((CARDS, 256), BF16),
         ),
-        in_specs=[vmem] * 10,
+        in_specs=[hbm] + [vmem] * 6 + [hbm, vmem, hbm],
         out_specs=(vmem, vmem),
         scratch_shapes=[
+            pltpu.VMEM((1024, 1024), BF16),
+            pltpu.VMEM((1024, 4, 256), BF16),
+            pltpu.VMEM((256, 1024), BF16),
             pltpu.VMEM((1024, 1024), BF16),
             pltpu.VMEM((256, 1024), BF16),
             pltpu.VMEM((2, 1024, 1024), BF16),
@@ -471,6 +484,7 @@
             pltpu.VMEM((1024, 256), BF16),
             pltpu.SemaphoreType.DMA((N_SEM,)),
             pltpu.SemaphoreType.DMA((N_SEM,)),
+            pltpu.SemaphoreType.DMA((3,)),
         ],
         compiler_params=pltpu.CompilerParams(
             collective_id=0, has_side_effects=True, vmem_limit_bytes=56 * 2**20

time: 96.7 us -> 96.3 us (level); the launches traced: 96.5 us -> 94.7 us
  Pallas kernels: 92.5 us -> 90.7 us
    pallas_call x1, Pallas kernels: 92.5 us -> 90.7 us  [shards(): pl.pallas_call(kernel, out_shape=(jax.ShapeDtypeStruct((1024, 256), BF16)...]
where the time goes in v6:
time: 96.3 us; the launch traced here: 94.7 us
  Pallas kernels  90.7 us (94%)
  local copies, waits for them, and re-layouts  3.34 us (3%)
    pallas_call x1, Pallas kernels, shards(): pl.pallas_call(kernel, out_shape=(jax.ShapeDtypeStruct((1024, 256), BF16)...  90.7 us
    unnamed x2, local copies, waits for them, and re-layouts  3.34 us

profile of v6, /device:TPU:1, one launch (start us, length us, event | category | flops | bytes accessed | tf_op | source)
XLA Modules:
  0.0 94.7 jit_solution(11378173272458748372)
XLA Ops:
  0.6 90.7 %hstu.1 = (bf16[1024,256]{1,0:T(8,128)(2,1)}, bf16[128,256]{1,0:T(8,128)(2,1)}) custom-call(bf16[1024,1024]{1,0:T(8,128)(2,1)} %x_hbm.1, bf16[128,1024]{1,0:T(8,128)(2,1)} %cx_ref.1, s32[8,128]{1,0:T(8,128)} %bitcast.6, s32[8,128]{1,0:T(8,128)} %bitcast.7, s32[1,128]{1,0:T(1,128)} %bitcast.10, s32[1,128]{1,0:T(1,128)} %bitcast.11, f32[1,1024]{1,0:T(1,128)} %bitcast.8, ...), custom_call_target="tpu_custom_call" | custom-call | tf_op jit(solution)/shard_map/hstu/pallas_call | solution.py:448
  91.3 1.9 %copy.14 = bf16[1024,256]{1,0:T(8,128)(2,1)} copy(bf16[1024,256]{1,0:T(8,128)(2,1)} %get-tuple-element.4) | data formatting | bytes 1048576
  93.2 1.5 %copy.15 = bf16[128,256]{1,0:T(8,128)(2,1)} copy(bf16[128,256]{1,0:T(8,128)(2,1)} %get-tuple-element.5) | data formatting | bytes 131072

commit v7 on v6

--- a/solution.py
+++ b/solution.py
@@ -414,8 +414,8 @@
     got[4] = stats_out(4, cattn[...])
     gate_hist(1)
     gate_hist(0)
+    moving[4] = gate_out(4, cattn[...], cp[:, 0:256], got[4])
     gate_forward(3, moving[3])
-    moving[4] = gate_out(4, cattn[...], cp[:, 0:256], got[4])
     for copy in into:
         copy.wait_recv()
     gate_forward(2, moving[2])

time: 96.3 us -> 96.3 us (level)
  no operation moved by 1% of the time
where the time goes in v7:
time: 96.3 us; the launch traced here: 94.7 us
  Pallas kernels  90.7 us (94%)
  local copies, waits for them, and re-layouts  3.34 us (3%)
    pallas_call x1, Pallas kernels, shards(): pl.pallas_call(kernel, out_shape=(jax.ShapeDtypeStruct((1024, 256), BF16)...  90.7 us
    unnamed x2, local copies, waits for them, and re-layouts  3.34 us

profile of v7, /device:TPU:1, one launch (start us, length us, event | category | flops | bytes accessed | tf_op | source)
XLA Modules:
  0.0 94.7 jit_solution(16871409882586102034)
XLA Ops:
  0.6 90.7 %hstu.1 = (bf16[1024,256]{1,0:T(8,128)(2,1)}, bf16[128,256]{1,0:T(8,128)(2,1)}) custom-call(bf16[1024,1024]{1,0:T(8,128)(2,1)} %x_hbm.1, bf16[128,1024]{1,0:T(8,128)(2,1)} %cx_ref.1, s32[8,128]{1,0:T(8,128)} %bitcast.6, s32[8,128]{1,0:T(8,128)} %bitcast.7, s32[1,128]{1,0:T(1,128)} %bitcast.10, s32[1,128]{1,0:T(1,128)} %bitcast.11, f32[1,1024]{1,0:T(1,128)} %bitcast.8, ...), custom_call_target="tpu_custom_call" | custom-call | tf_op jit(solution)/shard_map/hstu/pallas_call | solution.py:448
  91.3 1.9 %copy.14 = bf16[1024,256]{1,0:T(8,128)(2,1)} copy(bf16[1024,256]{1,0:T(8,128)(2,1)} %get-tuple-element.4) | data formatting | bytes 1048576
  93.2 1.5 %copy.15 = bf16[128,256]{1,0:T(8,128)(2,1)} copy(bf16[128,256]{1,0:T(8,128)(2,1)} %get-tuple-element.5) | data formatting | bytes 131072
